TPU v7x, 32 devices: a whole 2x2x4 slice. The times are simulated.
32 devices in a mesh: jobs: 2 (over x), clus: 16 (over z, y, core).
Axes of the slice: x: 2, y: 2, z: 4, core: 2. Of those that a mesh axis runs over, the one named last changes fastest.
Arguments:
- vertices: float32 [3, 65536], P(None, ('jobs', 'clus')), parts along dimension 1, may hold values from 0 to 17
- panel_vertices: int32 [3, 131072], P(None, ('jobs', 'clus')), parts along dimension 1, may hold values from 0 to 32767, as said below
- near_pairs: int32 [512, 4], P(('jobs', 'clus')), parts along dimension 0, may hold values from -1 to 255, as said below
- far_pairs: int32 [512, 32], P(('jobs', 'clus')), parts along dimension 0, may hold values from 0 to 255, as said below
- basis: float32 [32, 131072], P(None, ('jobs', 'clus')), parts along dimension 1, may hold values from -0.75 to 0.75
- krylov: float32 [16, 131072], P(None, ('jobs', 'clus')), parts along dimension 1, may hold values from -12 to 12
Outputs:
- next_basis: float32 [16, 131072], P(None, ('jobs', 'clus')), parts along dimension 1
- second_image: float32 [16, 131072], P(None, ('jobs', 'clus')), parts along dimension 1
There are 2 independent parts, one for each index of `jobs`. A program takes and returns all parts, laid end to end along the dimension named above; each array names one. Nothing has to cross between parts.
Inputs may be any that keep to these rules, and one draw needn't show every extreme that they name: `panel_vertices`: the vertices of a panel of cluster c are among vertices c * 128 to (c + 1) * 128 - 1. `near_pairs`: row c starts with c itself, then distinct clusters j with |j // 16 - c // 16| <= 1; live entries come first and -1 fills the rest; some row has all 4 slots live. `far_pairs`: row c holds 32 distinct clusters j with 2 <= |j // 16 - c // 16| <= 4.
All inputs are finite; a program needn't handle non-finite values.
Results may differ from a plain program's by a relative error of at most 0.0003.
Values sent between devices are 32-bit elements; how exact they have to be, the bound alone decides.
No kernel may reach another device: no remote copies, remote signals or barrier semaphores. Data moves between devices by JAX's collectives and lax.ppermute only.
A program may use at most 128 MiB of HBM per device.

v0:
```python
import functools

import jax
import jax.numpy as jnp
import numpy as np
from jax import lax
from jax.experimental import pallas as pl
from jax.experimental.pallas import tpu as pltpu
from jax.sharding import PartitionSpec as P

REACH = 4
SMOOTHING = 0.04
COULOMB = 2.0
PROXY_RADIUS = 0.6
LANES = 128
F32 = jnp.float32
BF16 = jnp.bfloat16


def proxy_offsets(points):
    counter = np.arange(points, dtype=np.float32)
    height = 1.0 - (2.0 * counter + 1.0) / points
    radial = np.sqrt(1.0 - height * height)
    azimuth = counter * 2.399963
    return PROXY_RADIUS * np.stack([radial * np.cos(azimuth), radial * np.sin(azimuth), height]).astype(np.float32)


def split(value):
    high = value.astype(BF16)
    return high, (value - high.astype(F32)).astype(BF16)


def stacked(value):
    return jnp.concatenate(split(value), axis=0)


def folded(value):
    half = value.shape[0] // 2
    return value[:half] + value[half:]


def dot_nt(left, right):
    return lax.dot_general(left, right, (((1,), (1,)), ((), ())), preferred_element_type=F32)


def dot_nn(left, right):
    return lax.dot_general(left, right, (((1,), (0,)), ((), ())), preferred_element_type=F32)


def quartered(value):
    half = value.shape[1] // 2
    value = folded(value)
    return value[:, 0:half] + value[:, half:]


def moments_of(weighted, basis_pieces):
    return quartered(dot_nt(stacked(weighted), basis_pieces))


def copies(pairs, sems):
    moves = [pltpu.make_async_copy(source, target, sems.at[i]) for i, (source, target) in enumerate(pairs)]
    for move in moves:
        move.start()
    return moves


def pair_list(near, position, clusters):
    block = lax.div(near, clusters) - position
    place = (1 - block * (1 - 2 * lax.rem(position, 2))) * clusters + lax.rem(near, clusters)
    place = place.astype(F32)
    across = lax.broadcasted_iota(jnp.int32, (clusters, clusters), 1)
    down = lax.broadcasted_iota(jnp.int32, (clusters, clusters), 0)
    upright = lambda value: jnp.sum(jnp.where(across == down, value, 0.0), axis=1, keepdims=True)
    row = lax.broadcasted_iota(jnp.int32, (clusters, LANES), 1).astype(F32)
    target = lax.broadcasted_iota(jnp.int32, (clusters, 1), 0).astype(F32)
    rows = lax.broadcasted_iota(jnp.int32, (8, LANES), 0)
    out = jnp.zeros((8, LANES), F32)
    for which in range(2):
        here = place >= 2.0 * clusters if which else place < 2.0 * clusters
        live = jnp.where(here & (near >= 0), 1.0, 0.0)
        counts = sum(live[k:k + 1] for k in range(near.shape[0]))
        first = jnp.sum(jnp.where(across < down, counts, 0.0), axis=1, keepdims=True)
        found = jnp.zeros((clusters, LANES), F32)
        for k in range(near.shape[0]):
            alive = upright(live[k:k + 1])
            hit = jnp.where(row == first, alive, 0.0)
            found = found + hit * (target * 64 + upright(place[k:k + 1]) - 2.0 * clusters * which)
            first = first + alive
        count = jnp.sum(counts, axis=1, keepdims=True)
        found = jnp.where(row[0:1] < count, jnp.sum(found, axis=0, keepdims=True), (2.0 - which) * clusters)
        out = jnp.where(rows == which, found, jnp.where(rows == 2 + which, count, out))
    return out.astype(jnp.int32)


def prepare_kernel(cl, vcl, rank, position_ref, vertices_hbm, corners_hbm, krylov_hbm, basis_hbm, far_hbm, near_hbm, offsets_hbm,
                   payload_ref, area_ref, center_ref, at_ref, pairs_ref, basis_ref, krylov_ref, offsets_ref,
                   vertices_ref, corners_ref, raw_ref, far_ref, near_ref, mesh_ref, local_ref, sems):
    moves = copies((
        (vertices_hbm, vertices_ref), (corners_hbm, corners_ref), (krylov_hbm, krylov_ref), (basis_hbm, raw_ref),
        (far_hbm, far_ref), (near_hbm, near_ref), (offsets_hbm, offsets_ref),
    ), sems)
    rhs, panels = krylov_ref.shape
    clusters = panels // cl
    parts = cl // LANES
    moves[0].wait()
    for c in range(clusters):
        mesh_ref[3 * c:3 * c + 3, :] = vertices_ref[:, c * vcl:(c + 1) * vcl]
    moves[1].wait()
    for i in range(clusters * parts):
        local_ref[3 * i:3 * i + 3, :] = corners_ref[:, i * LANES:(i + 1) * LANES]
    first = position_ref[0] * (vcl * clusters) + vcl * lax.broadcasted_iota(jnp.int32, (clusters, LANES), 0)
    tables = [mesh_ref[pl.ds(k, clusters, stride=3), :] for k in range(3)]
    sums = [None] * 3
    for h in range(parts):
        local = [local_ref[pl.ds(3 * h + m, clusters, stride=3 * parts), :] - first for m in range(3)]
        corner = [[jnp.take_along_axis(tables[k], local[m], axis=1, mode="promise_in_bounds") for k in range(3)] for m in range(3)]
        for k in range(3):
            middle = (corner[0][k] + corner[1][k] + corner[2][k]) / 3.0
            payload_ref[:, panels + k * cl + h * LANES:panels + k * cl + (h + 1) * LANES] = middle
            sums[k] = middle if h == 0 else sums[k] + middle
        one = [corner[1][k] - corner[0][k] for k in range(3)]
        two = [corner[2][k] - corner[0][k] for k in range(3)]
        normal = [one[1] * two[2] - one[2] * two[1], one[2] * two[0] - one[0] * two[2], one[0] * two[1] - one[1] * two[0]]
        area_ref[:, h * LANES:(h + 1) * LANES] = 0.5 * jnp.sqrt(normal[0] * normal[0] + normal[1] * normal[1] + normal[2] * normal[2])
    span = clusters * rank
    table = panels + 3 * cl
    mine = lax.broadcasted_iota(jnp.int32, (clusters, span), 1) // rank == lax.broadcasted_iota(jnp.int32, (clusters, span), 0)
    half = span // 2
    payload_ref[:, table + span:] = jnp.zeros_like(payload_ref[:, table + span:])
    for k in range(3):
        center = jnp.sum(sums[k], axis=1, keepdims=True) / cl
        center_ref[:, k * LANES:(k + 1) * LANES] = jnp.broadcast_to(center, (clusters, LANES))
        row = jnp.sum(jnp.where(mine, center, 0.0), axis=0, keepdims=True)
        payload_ref[k:k + 1, table + span:] = row[:, 0:half]
        payload_ref[8 + k:9 + k, table + span:] = row[:, half:]
    moves[2].wait()
    moves[3].wait()
    for c in range(clusters):
        lanes = slice(c * cl, (c + 1) * cl)
        basis_ref[:, lanes] = stacked(raw_ref[:, lanes])
        charges = area_ref[c:c + 1, :] * krylov_ref[:, lanes]
        payload_ref[:, lanes] = charges
        payload_ref[:, table + c * rank:table + (c + 1) * rank] = moments_of(charges, basis_ref[:, lanes])
    moves[4].wait()
    far = far_ref[...]
    step = (lax.div(far, clusters) - position_ref[0]) * (1 - 2 * lax.rem(position_ref[0], 2))
    block = jnp.where(step < 0, step + REACH, step + REACH - 3)
    per = LANES // rank
    turn = lax.rem(lax.broadcasted_iota(jnp.int32, far.shape, 1) - far + per * clusters * 2 ** 16, per)
    at_ref[...] = (turn * 6 + block) * (span // LANES) + lax.div(lax.rem(far, clusters), per)
    moves[5].wait()
    pairs_ref[...] = pair_list(near_ref[...], position_ref[0], clusters)
    moves[6].wait()


def columns_of(payload_ref, panels, c, cl, columns_ref, at):
    rows = [payload_ref[c:c + 1, panels + k * cl:panels + (k + 1) * cl] for k in range(3)]
    upright = jnp.transpose(jnp.concatenate(rows * 2 + rows[:2], axis=0))
    for k in range(3):
        columns_ref[at, k] = jnp.broadcast_to(upright[:, k:k + 1], (cl, LANES))


def near_block(columns, source, cl, out_ref, at):
    for h in range(cl // LANES):
        lanes = slice(h * LANES, (h + 1) * LANES)
        gap = [columns[k] - source(k, h) for k in range(3)]
        square = gap[0] * gap[0] + gap[1] * gap[1] + gap[2] * gap[2]
        high, low = split(lax.rsqrt(square + SMOOTHING))
        out_ref[at, 0:cl, lanes] = high
        out_ref[at, cl:2 * cl, lanes] = low


def near_product(pieces, block_ref, at, cl):
    return dot_nt(pieces, block_ref[at, 0:cl, :]) + dot_nt(pieces, block_ref[at, cl:2 * cl, :])


def fill_charges(pieces_ref, blocks, clusters, cl):
    for b, ref in enumerate(blocks):
        for c in range(clusters):
            pieces_ref[b * clusters + c] = stacked(ref[:, c * cl:(c + 1) * cl])
    pieces_ref[len(blocks) * clusters] = jnp.zeros_like(pieces_ref[0])


def pair_at(pairs_ref, which, i):
    pair = pairs_ref[which, i]
    return lax.shift_right_logical(pair, 6), lax.bitwise_and(pair, 63)


def near_kernel(cl, which, number, pairs_ref, *refs):
    blocks = refs[:number]
    if which:
        columns_ref, start_ref, even_ref, odd_ref, near_out_ref, pieces_ref, sources_ref, total_ref = refs[number:]
    else:
        even_ref, odd_ref, near_out_ref, columns_ref, tail_ref, pieces_ref, sources_ref, total_ref = refs[number:]
        tail_ref[...] = blocks[1][:, blocks[1].shape[1] - tail_ref.shape[1]:]
    panels = near_out_ref.shape[1]
    clusters = panels // cl
    steps = (pairs_ref[2 + which, 0] + 1) // 2
    sources_ref[number * clusters] = jnp.zeros_like(sources_ref[0])
    for b, ref in enumerate(blocks):
        for c in range(clusters):
            for k in range(3):
                sources_ref[b * clusters + c, k:k + 1, :] = ref[c:c + 1, panels + k * cl:panels + (k + 1) * cl]
    fill_charges(pieces_ref, blocks, clusters, cl)
    for c in range(clusters):
        if not which:
            columns_of(blocks[1], panels, c, cl, columns_ref, c)
        total_ref[c] = jnp.zeros_like(total_ref[c])
    odd_ref[0] = jnp.zeros_like(odd_ref[0])

    def build(ref, at, i):
        c, j = pair_at(pairs_ref, which, i)
        source = lambda k, h: sources_ref[j, k:k + 1, h * LANES:(h + 1) * LANES]
        near_block([columns_ref[c, k] for k in range(3)], source, cl, ref, at)

    def product(ref, at, i):
        return near_product(pieces_ref[pair_at(pairs_ref, which, i)[1]], ref, at, cl)

    def add(i, part):
        total_ref[pair_at(pairs_ref, which, i)[0]] += part

    def step(m, _):
        before = jnp.maximum(2 * m - 1, 0)
        part = product(odd_ref, m, before)
        build(even_ref, m, 2 * m)
        add(before, part)
        part = product(even_ref, m, 2 * m)
        build(odd_ref, m + 1, 2 * m + 1)
        add(2 * m, part)
        return 0

    lax.fori_loop(0, steps, step, 0)
    last = jnp.maximum(2 * steps - 1, 0)
    add(last, product(odd_ref, steps, last))
    for c in range(clusters):
        lanes = slice(c * cl, (c + 1) * cl)
        near = folded(total_ref[c])
        near_out_ref[:, lanes] = start_ref[:, lanes] + near if which else near


def near_again_kernel(cl, which, number, pairs_ref, *refs):
    blocks = refs[:number]
    if which:
        start_ref, even_ref, odd_ref, near_out_ref, pieces_ref, total_ref = refs[number:]
    else:
        even_ref, odd_ref, near_out_ref, tail_ref, pieces_ref, total_ref = refs[number:]
        tail_ref[...] = blocks[1][:, blocks[1].shape[1] - tail_ref.shape[1]:]
    clusters = near_out_ref.shape[1] // cl
    fill_charges(pieces_ref, blocks, clusters, cl)
    for c in range(clusters):
        total_ref[c] = jnp.zeros_like(total_ref[c])
    count = pairs_ref[2 + which, 0]

    def step(m, _):
        parts = []
        for w in range(4):
            i = 4 * m + w
            at = jnp.where(i < count, i // 2, 0) + w % 2
            parts.append(near_product(pieces_ref[pair_at(pairs_ref, which, i)[1]], (even_ref, odd_ref)[w % 2], at, cl))
        for w in range(4):
            total_ref[pair_at(pairs_ref, which, 4 * m + w)[0]] += parts[w]
        return 0

    lax.fori_loop(0, (count + 3) // 4, step, 0)
    for c in range(clusters):
        lanes = slice(c * cl, (c + 1) * cl)
        near = folded(total_ref[c])
        near_out_ref[:, lanes] = start_ref[:, lanes] + near if which else near


def load_window(tables, clusters, rank, pieces_ref, middle_ref):
    per = LANES // rank
    span = clusters * rank
    count = pieces_ref.shape[0] // per
    groups = span // LANES
    for at in range(count):
        (ref, first), g = tables[at // groups], at % groups
        tile = ref[:, first + g * LANES:first + (g + 1) * LANES]
        for s in range(per):
            pieces_ref[s * count + at] = stacked(pltpu.roll(tile, s * rank, 1) if s else tile)
        if middle_ref is not None:
            half = groups // 2
            row, lane = 8 * (g // half), first + span + g % half * LANES
            tile = ref[row:row + 8, lane:lane + LANES]
            for s in range(per):
                middle_ref[s * count + at] = pltpu.roll(tile, s * rank, 1) if s else tile


def six_tables(width, second_ref, other_ref, third_ref):
    return (second_ref, width), (second_ref, 0), (other_ref, other_ref.shape[1] - width), (third_ref, 2 * width), (third_ref, width), (third_ref, 0)


def pick(source_ref, at_ref, c, g, per, lane):
    row = None
    for u in range(per):
        take = source_ref[at_ref[c, g * per + u]]
        row = take if row is None else jnp.where(lane == u, take, row)
    return row


def far_fields(gathered_ref, coupling_ref, fields_ref):
    for c in range(gathered_ref.shape[0]):
        field = quartered(dot_nt(gathered_ref[c], coupling_ref[c]))
        fields_ref[c] = stacked(jnp.concatenate([field, field], axis=1))


def far_potential(fields_ref, c, basis):
    return folded(dot_nn(fields_ref[c], basis))


def image_kernel(cl, rank, at_ref, second_ref, other_ref, third_ref, center_ref, area_ref, near_ref, basis_ref, krylov_ref, offsets_ref,
                 image_ref, payload_ref, coupling_ref, pieces_ref, middle_ref, gathered_ref, fields_ref):
    rhs, panels = near_ref.shape
    clusters = panels // cl
    per = LANES // rank
    span = clusters * rank
    load_window(six_tables(span + span // 2, second_ref, other_ref, third_ref), clusters, rank, pieces_ref, middle_ref)
    lane = lax.broadcasted_iota(jnp.int32, (1, LANES), 1) // rank
    for c in range(clusters):
        mine = [offsets_ref[3, k:k + 1, :] - center_ref[c:c + 1, k * LANES:(k + 1) * LANES] for k in range(3)]
        for g in range(at_ref.shape[1] // per):
            lanes = slice(g * LANES, (g + 1) * LANES)
            gathered_ref[c, :, lanes] = pick(pieces_ref, at_ref, c, g, per, lane)
            center = pick(middle_ref, at_ref, c, g, per, lane)
            gap = [(center[k:k + 1] + mine[k]) - offsets_ref[k] for k in range(3)]
            high, low = split(lax.rsqrt(gap[0] * gap[0] + gap[1] * gap[1] + gap[2] * gap[2] + SMOOTHING))
            coupling_ref[c, 0:rank, lanes] = high
            coupling_ref[c, rank:2 * rank, lanes] = low
    far_fields(gathered_ref, coupling_ref, fields_ref)
    squared = correlation = jnp.zeros((rhs, cl), F32)
    for c in range(clusters):
        lanes = slice(c * cl, (c + 1) * cl)
        basis = basis_ref[:, lanes]
        area = area_ref[c:c + 1, :]
        image = COULOMB * area * (near_ref[:, lanes] + far_potential(fields_ref, c, basis))
        charges = area * image
        image_ref[:, lanes] = image
        payload_ref[:, lanes] = charges
        payload_ref[:, panels + c * rank:panels + (c + 1) * rank] = moments_of(charges, basis)
        krylov = krylov_ref[:, lanes]
        squared = squared + krylov * krylov
        correlation = correlation + krylov * image
    squared = jnp.sum(squared, axis=1, keepdims=True)
    correlation = jnp.sum(correlation, axis=1, keepdims=True)
    local = ratio(correlation, squared)
    residual = image_ref[...] - local * krylov_ref[...]
    payload_ref[:, panels + span:] = in_lanes(squared, correlation, jnp.sum(residual * residual, axis=1, keepdims=True), local)


def finish_kernel(cl, rank, total, at_ref, one_ref, two_ref, second_table_ref, other_ref, third_ref, near_ref, area_ref, image_ref, coupling_ref, basis_ref, krylov_ref,
                  next_hbm, second_hbm, pieces_ref, gathered_ref, fields_ref, next_ref, second_ref, sems):
    clusters = near_ref.shape[1] // cl
    per = LANES // rank
    squared, correlation, energy, local = merged([one_ref[...], two_ref[...]])
    projection = correlation / (squared + 1e-06)
    gap = projection - local
    scaling = 1.0 / jnp.sqrt((energy + gap * gap * squared) / total + 1e-06)
    next_ref[...] = (image_ref[...] - projection * krylov_ref[...]) * scaling
    moves = copies(((next_ref, next_hbm),), sems)
    load_window(six_tables(clusters * rank, second_table_ref, other_ref, third_ref), clusters, rank, pieces_ref, None)
    lane = lax.broadcasted_iota(jnp.int32, (1, LANES), 1) // rank
    for c in range(clusters):
        for g in range(at_ref.shape[1] // per):
            gathered_ref[c, :, g * LANES:(g + 1) * LANES] = pick(pieces_ref, at_ref, c, g, per, lane)
    far_fields(gathered_ref, coupling_ref, fields_ref)
    for c in range(clusters):
        lanes = slice(c * cl, (c + 1) * cl)
        image = COULOMB * area_ref[c:c + 1, :] * (near_ref[:, lanes] + far_potential(fields_ref, c, basis_ref[:, lanes]))
        second_ref[:, lanes] = (image - projection * image_ref[:, lanes]) * scaling
    moves.append(pltpu.make_async_copy(second_ref, second_hbm, sems.at[1]))
    moves[1].start()
    moves[0].wait()
    moves[1].wait()


def ratio(correlation, squared):
    return jnp.where(squared > 0, correlation / jnp.where(squared > 0, squared, 1.0), 0.0)


def in_lanes(*columns):
    lane = lax.broadcasted_iota(jnp.int32, (columns[0].shape[0], LANES), 1)
    out = columns[-1]
    for i, column in enumerate(columns[:-1]):
        out = jnp.where(lane == i, column, out)
    return out


def merged(groups):
    squared = sum(group[:, 0:1] for group in groups)
    correlation = sum(group[:, 1:2] for group in groups)
    local = ratio(correlation, squared)
    energy = 0.0
    for group in groups:
        gap = local - group[:, 3:4]
        energy = energy + (group[:, 2:3] + gap * gap * group[:, 0:1])
    return squared, correlation, energy, local


def merge_kernel(one_ref, two_ref, out_ref):
    out_ref[...] = in_lanes(*merged([ref[:, ref.shape[1] - LANES:] for ref in (one_ref, two_ref)]))


def call(kernel, outs, scratch, memory, *args, limit=6, us=1.0):
    spaces = {"s": pltpu.SMEM, "v": pltpu.VMEM, "p": pltpu.VMEM, "h": pltpu.HBM}
    ins, out_spaces = memory.split(">")
    pinned = {"h": pltpu.HBM, "p": pltpu.VMEM}
    return pl.pallas_call(
        kernel,
        out_shape=[pltpu.VMEM(*out) if m == "p" else jax.ShapeDtypeStruct(*out) for m, out in zip(out_spaces, outs)],
        in_specs=[pl.BlockSpec(memory_space=spaces[m]) for m in ins],
        out_specs=[pl.BlockSpec(memory_space=spaces[m]) for m in out_spaces],
        scratch_shapes=scratch,
        compiler_params=pltpu.CompilerParams(vmem_limit_bytes=limit * 2 ** 20),
        cost_estimate=pl.CostEstimate(flops=int(us * 5e8), bytes_accessed=int(us * 3.6e6), transcendentals=0),
    )(*(pltpu.with_memory_space_constraint(a, pinned[m]) if m in pinned else a for m, a in zip(ins, args)))


def body(vertices, panel_vertices, near_pairs, far_pairs, basis, krylov):
    clusters, slots = near_pairs.shape
    partners = far_pairs.shape[1]
    rhs, panels = krylov.shape
    rank = basis.shape[0]
    cl = panels // clusters
    vcl = vertices.shape[1] // clusters
    span = clusters * rank
    per = LANES // rank
    devices = lax.axis_size("clus")
    position = lax.axis_index("clus").reshape(1).astype(jnp.int32)
    offsets = proxy_offsets(rank)
    flat = np.concatenate([np.tile(offsets, (1, per)), np.zeros((rank - 3, LANES), np.float32)])
    offsets = jnp.asarray(np.concatenate([np.broadcast_to(offsets[:, :, None], (3, rank, LANES)), flat[None]]))
    width = span + span // 2
    pairing = [(i, i + 1 - 2 * (i % 2)) for i in range(devices)]
    bridging = [(i, i - 1 + 2 * (i % 2)) for i in range(1, devices - 1)] + [(0, 0), (devices - 1, devices - 1)]
    second = [(i, (i + 3 * (2 * (i % 2) - 1)) % devices) for i in range(devices)]
    third = [(i, i + 4 * (2 * (i % 2) - 1)) for i in range(1, devices - 1)] + [(0, 3), (devices - 1, devices - 4)]
    third = [(i, j % devices) for i, j in third]

    def move(value, pairs):
        return lax.ppermute(value, "clus", pairs)

    def exchange(value, first, width):
        mine = value[:, first:first + width]
        partner = move(value, pairing)
        pair = jnp.concatenate([mine, partner[:, first:first + width]], axis=1)
        other = move(jnp.concatenate([value[:, :first], pair], axis=1), bridging)
        return partner, other, move(pair, second)

    def last_exchange(tail, other, width):
        return move(jnp.concatenate([tail[:, :width], other[:, other.shape[1] - 2 * width:]], axis=1), third)

    whole = ((rhs, panels), F32)
    payload, area, centers, at, pairs, basis, krylov, offsets = call(
        functools.partial(prepare_kernel, cl, vcl, rank),
        [
            ((rhs, panels + 3 * cl + width), F32), ((clusters, cl), F32), ((clusters, 3 * LANES), F32),
            (far_pairs.shape, jnp.int32), ((8, LANES), jnp.int32), ((2 * rank, panels), BF16), whole, (offsets.shape, F32),
        ],
        [
            pltpu.VMEM(vertices.shape, F32),
            pltpu.VMEM(panel_vertices.shape, jnp.int32),
            pltpu.VMEM(basis.shape, F32),
            pltpu.VMEM(far_pairs.shape, jnp.int32),
            pltpu.VMEM((slots, clusters), jnp.int32),
            pltpu.VMEM((3 * clusters, vcl), F32),
            pltpu.VMEM((3 * panels // LANES, LANES), jnp.int32),
            pltpu.SemaphoreType.DMA((7,)),
        ],
        "shhhhhhh>vvvvvppp",
        position, vertices, panel_vertices, krylov, basis, far_pairs, near_pairs.T, offsets,
        us=1.5,
    )
    partner, other, two = exchange(payload, panels + 3 * cl, width)
    total = pltpu.VMEM((clusters, 2 * rhs, cl), F32)

    def kept(most):
        return [(((most + 1) // 2 + 1, 2 * cl, cl), BF16)] * 2

    def pieces(number):
        return pltpu.VMEM((number * clusters + 1, 2 * rhs, cl), BF16)

    def sources(number):
        return pltpu.VMEM((number * clusters + 1, 8, cl), F32)

    even, odd, near, columns, tail = call(
        functools.partial(near_kernel, cl, 0, 2),
        [*kept(clusters * slots), whole, ((clusters, 3, cl, LANES), F32), ((rhs, width), F32)],
        [pieces(2), sources(2), total],
        "svv>ppvpv",
        pairs, partner, payload,
        us=8.0,
    )
    three = last_exchange(tail, other, width)
    even_other, odd_other, near = call(
        functools.partial(near_kernel, cl, 1, 1),
        [*kept(clusters * (slots - 1)), whole],
        [pieces(1), sources(1), total],
        "svpv>ppv",
        pairs, other, columns, near,
        us=3.0,
    )
    tiles = 6 * per * span // LANES
    window = pltpu.VMEM((tiles, 2 * rhs, LANES), BF16)
    gathered = pltpu.VMEM((clusters, 2 * rhs, partners * rank), BF16)
    fields = pltpu.VMEM((clusters, 2 * rhs, 2 * rank), BF16)
    image, payload, coupling = call(
        functools.partial(image_kernel, cl, rank),
        [whole, ((rhs, panels + span + LANES), F32), ((clusters, 2 * rank, partners * rank), BF16)],
        [window, pltpu.VMEM((tiles, 8, LANES), F32), gathered, fields],
        "svvvvvvppp>vvp",
        at, two, other, three, centers, area, near, basis, krylov, offsets,
        us=4.5,
    )
    partner, other, two = exchange(payload, panels, span)
    near, one = call(
        functools.partial(near_again_kernel, cl, 0, 2),
        [whole, ((rhs, span + LANES), F32)],
        [pieces(2), total],
        "svvpp>vv",
        pairs, partner, payload, even, odd,
        us=2.5,
    )
    three = last_exchange(one, other, span)
    many = partner
    size = 2
    while size < devices:
        (one,) = call(merge_kernel, [((rhs, LANES), F32)], [], "vv>v", one, many, us=0.3)
        many = move(one, [(i, (i + size) % devices) for i in range(devices)])
        size = 2 * size
    (near,) = call(
        functools.partial(near_again_kernel, cl, 1, 1),
        [whole],
        [pieces(1), total],
        "svvpp>v",
        pairs, other, near, even_other, odd_other,
        us=2.0,
    )
    here = pltpu.VMEM((rhs, panels), F32)
    return tuple(call(
        functools.partial(finish_kernel, cl, rank, panels * devices),
        [whole, whole],
        [window, gathered, fields, here, here, pltpu.SemaphoreType.DMA((2,))],
        "svvvvvvvvppp>hh",
        at, one, many, two, other, three, near, area, image, coupling, basis, krylov,
        us=3.0,
    ))


def solution(mesh):
    whole = P(None, ("jobs", "clus"))
    rows = P(("jobs", "clus"), None)
    return jax.shard_map(
        body,
        mesh=mesh,
        in_specs=(whole, whole, rows, rows, whole, whole),
        out_specs=(whole, whole),
        check_vma=False,
    )
```

profile of v0, /device:TPU:0, one launch (start us, length us, event | category | flops | bytes accessed | tf_op | source)
XLA Modules:
  0.0 63.1 jit_solution(5593117977120603119)
XLA Ops:
  0.6 1.8 %shard_map.86 = (f32[16,5632]{1,0:T(8,128)S(1)}, f32[16,256]{1,0:T(8,128)S(1)}, f32[16,384]{1,0:T(8,128)S(1)}, s32[16,32]{1,0:T(8,128)S(1)}, s32[8,128]{1,0:T(8,...) custom-call(s32[1]{0:T(128)} %bitcast.position_ref, ...), custom_call_target="tpu_custom_call" | custom-call | flops 750000000 | bytes 5400000 | tf_op jit(solution)/shard_map/pallas_call | solution.py:407
  2.4 0.5 collective-permute-start
  3.0 1.3 %collective-permute-done.refs_0_ = f32[16,5632]{1,0:T(8,128)S(1)} collective-permute-done((f32[16,5632]{1,0:T(8,128)S(1)}, f32[16,5632]{1,0:T(8,128)S(1)}, u32[]{:S(2)}, u32[]{:S(2)}) %collective-permute-start) | collective-permute-done | bytes 360480 | tf_op jit(solution)/shard_map/ppermute | solution.py:440
  4.3 0.7 %collective-permute-start.2 = (f32[16,6400]{1,0:T(8,128)S(1)}, f32[16,6400]{1,0:T(8,128)S(1)}, u32[]{:S(2)}, u32[]{:S(2)}) collective-permute-start(f32[16,6400]{1,0:T(8,128)S(1)} %pad_maximum_fusion), channel_id=1, source_target_pairs={{1,2},{2,1},{3,4},{4,3},{5,6},{6,5},{7,8},{8,7},{9,10},{10,9},{11,... | collective-permute-start | bytes 1228808 | tf_op jit(solution)/shard_map/ppermute | solution.py:440
  5.0 14.5 %shard_map.87 = (bf16[33,512,256]{2,1,0:T(8,128)(2,1)S(1)}, bf16[33,512,256]{2,1,0:T(8,128)(2,1)S(1)}, f32[16,4096]{1,0:T(8,128)S(1)}, f32[16,3,256,128]{3,2,1,0:T(8,128)S(1)}, f32[16,768]{1,0:T(8,128)S(1)}) custom-call(s32[8,128]{1,0:T(8,128)S(1)} %get-tuple-element.24.pairs_ref, f32[16,5632]{1,0:T(8,128)S(1)} %collective-permute-done.refs_0_, ...), custom_call_target="tpu_custom_call" | custom-call | flops 4000000000 | bytes 28800000 | tf_op jit(solution)/shard_map/pallas_call | solution.py:407
  19.5 0.0 collective-permute-done.2.refs_0_.other_ref
  19.5 1.3 %collective-permute-start.3 = (f32[16,2304]{1,0:T(8,128)S(1)}, f32[16,2304]{1,0:T(8,128)S(1)}, u32[]{:S(2)}, u32[]{:S(2)}) collective-permute-start(f32[16,2304]{1,0:T(8,128)S(1)} %pad_maximum_fusion.2), channel_id=1, source_target_pairs={{1,5},{2,14},{3,7},{4,0},{5,9},{6,2},{7,11},{8,4},{9,13},{10,6},{1... | collective-permute-start | bytes 442376 | tf_op jit(solution)/shard_map/ppermute | solution.py:440
  20.9 4.1 %collective-permute-start.1 = (f32[16,1536]{1,0:T(8,128)S(1)}, f32[16,1536]{1,0:T(8,128)S(1)}, u32[]{:S(2)}, u32[]{:S(2)}) collective-permute-start(f32[16,1536]{1,0:T(8,128)S(1)} %pad_maximum_fusion.3), channel_id=1, source_target_pairs={{0,13},{1,4},{2,15},{3,6},{4,1},{5,8},{6,3},{7,10},{8,5},{9,12},{1... | collective-permute-start | bytes 294920 | tf_op jit(solution)/shard_map/ppermute | solution.py:440
  25.0 0.9 %shard_map.88 = (bf16[25,512,256]{2,1,0:T(8,128)(2,1)S(1)}, bf16[25,512,256]{2,1,0:T(8,128)(2,1)S(1)}, f32[16,4096]{1,0:T(8,128)S(1)}) custom-call(s32[8,128]{1,0:T(8,128)S(1)} %get-tuple-element.24.pairs_ref, f32[16,6400]{1,0:T(8,128)S(1)} %collective-permute-done.2.refs_0_.other_ref, f32[16,3,256,128]{3,2,1,0:T(8,128)S(1)} %get-tuple-element.29.refs_1_, ...), custom_call_target="tpu_custom_call" | custom-call | flops 1500000000 | bytes 10800000 | tf_op jit(solution)/shard_map/pallas_call | solution.py:407
  25.9 4.8 %collective-permute-done.1.second_ref = f32[16,1536]{1,0:T(8,128)S(1)} collective-permute-done((f32[16,1536]{1,0:T(8,128)S(1)}, f32[16,1536]{1,0:T(8,128)S(1)}, u32[]{:S(2)}, u32[]{:S(2)}) %collective-permute-start.1) | collective-permute-done | bytes 98336 | tf_op jit(solution)/shard_map/ppermute | solution.py:440
  30.7 0.0 collective-permute-done.3.third_ref
  30.7 4.3 %shard_map.89 = (f32[16,4096]{1,0:T(8,128)S(1)}, f32[16,4736]{1,0:T(8,128)S(1)}, bf16[16,64,1024]{2,1,0:T(8,128)(2,1)S(1)}) custom-call(s32[16,32]{1,0:T(8,128)S(1)} %get-tuple-element.23.at_ref, f32[16,1536]{1,0:T(8,128)S(1)} %collective-permute-done.1.second_ref, f32[16,6400]{1,0:T(8,128)S(1)} %collective-permute-done.2.refs_0_.other_ref, ...), custom_call_target="tpu_custom_call" | custom-call | flops 2249999872 | bytes 16200000 | tf_op jit(solution)/shard_map/pallas_call | solution.py:407
  35.0 0.1 collective-permute-start.4
  35.1 1.6 %collective-permute-done.4.refs_0_.two_ref = f32[16,4736]{1,0:T(8,128)S(1)} collective-permute-done((f32[16,4736]{1,0:T(8,128)S(1)}, f32[16,4736]{1,0:T(8,128)S(1)}, u32[]{:S(2)}, u32[]{:S(2)}) %collective-permute-start.4) | collective-permute-done | bytes 303136 | tf_op jit(solution)/shard_map/ppermute | solution.py:440
  36.7 0.7 %collective-permute-start.9 = (f32[16,5120]{1,0:T(8,128)S(1)}, f32[16,5120]{1,0:T(8,128)S(1)}, u32[]{:S(2)}, u32[]{:S(2)}) collective-permute-start(f32[16,5120]{1,0:T(8,128)S(1)} %pad_maximum_fusion.1), channel_id=1, source_target_pairs={{1,2},{2,1},{3,4},{4,3},{5,6},{6,5},{7,8},{8,7},{9,10},{10,9},{11,... | collective-permute-start | bytes 983048 | tf_op jit(solution)/shard_map/ppermute | solution.py:440
  37.4 5.3 %shard_map.90 = (f32[16,4096]{1,0:T(8,128)S(1)}, f32[16,640]{1,0:T(8,128)S(1)}) custom-call(s32[8,128]{1,0:T(8,128)S(1)} %get-tuple-element.24.pairs_ref, f32[16,4736]{1,0:T(8,128)S(1)} %collective-permute-done.4.refs_0_.two_ref, f32[16,4736]{1,0:T(8,128)S(1)} %get-tuple-element.35.refs_1_, bf16[33,512,256]{2,1,0:T(8,128)(2,1)S(1)} %get-tuple-element.36.refs_2_, ...), custom_call_target="tpu_custom_call" | custom-call | flops 1250000000 | bytes 9000000 | tf_op jit(solution)/shard_map/pallas_call | solution.py:407
  42.7 0.3 shard_map.91.one_ref
  42.9 2.2 %collective-permute-start.5 = (f32[16,128]{1,0:T(8,128)S(1)}, f32[16,128]{1,0:T(8,128)S(1)}, u32[]{:S(2)}, u32[]{:S(2)}) collective-permute-start(f32[16,128]{1,0:T(8,128)S(1)} %shard_map.91.one_ref), channel_id=1, source_target_pairs={{0,2},{1,3},{2,4},{3,5},{4,6},{5,7},{6,8},{7,9},{8,10},{9,11},{10,... | collective-permute-start | bytes 24584 | tf_op jit(solution)/shard_map/ppermute | solution.py:440
  45.1 1.0 %collective-permute-start.8 = (f32[16,1024]{1,0:T(8,128)S(1)}, f32[16,1024]{1,0:T(8,128)S(1)}, u32[]{:S(2)}, u32[]{:S(2)}) collective-permute-start(f32[16,1024]{1,0:T(8,128)S(1)} %pad_maximum_fusion.5), channel_id=1, source_target_pairs={{0,13},{1,4},{2,15},{3,6},{4,1},{5,8},{6,3},{7,10},{8,5},{9,12},{1... | collective-permute-start | bytes 196616 | tf_op jit(solution)/shard_map/ppermute | solution.py:440
  46.1 3.2 %collective-permute-done.5.two_ref = f32[16,128]{1,0:T(8,128)S(1)} collective-permute-done((f32[16,128]{1,0:T(8,128)S(1)}, f32[16,128]{1,0:T(8,128)S(1)}, u32[]{:S(2)}, u32[]{:S(2)}) %collective-permute-start.5) | collective-permute-done | bytes 8224 | tf_op jit(solution)/shard_map/ppermute | solution.py:440
  49.3 0.3 shard_map.92.one_ref
  49.6 0.0 collective-permute-start.6
  49.6 0.0 collective-permute-done.9.refs_0_.other_ref
  49.6 0.8 %collective-permute-start.10 = (f32[16,1536]{1,0:T(8,128)S(1)}, f32[16,1536]{1,0:T(8,128)S(1)}, u32[]{:S(2)}, u32[]{:S(2)}) collective-permute-start(f32[16,1536]{1,0:T(8,128)S(1)} %pad_maximum_fusion.4), channel_id=1, source_target_pairs={{1,5},{2,14},{3,7},{4,0},{5,9},{6,2},{7,11},{8,4},{9,13},{10,6},{1... | collective-permute-start | bytes 294920 | tf_op jit(solution)/shard_map/ppermute | solution.py:440
  50.4 4.6 %collective-permute-done.6.two_ref = f32[16,128]{1,0:T(8,128)S(1)} collective-permute-done((f32[16,128]{1,0:T(8,128)S(1)}, f32[16,128]{1,0:T(8,128)S(1)}, u32[]{:S(2)}, u32[]{:S(2)}) %collective-permute-start.6) | collective-permute-done | bytes 8224 | tf_op jit(solution)/shard_map/ppermute | solution.py:440
  55.1 0.3 shard_map.93.one_ref
  55.4 0.0 collective-permute-start.7
  55.4 0.7 %shard_map.94.near_ref = f32[16,4096]{1,0:T(8,128)S(1)} custom-call(s32[8,128]{1,0:T(8,128)S(1)} %get-tuple-element.24.pairs_ref, f32[16,5120]{1,0:T(8,128)S(1)} %collective-permute-done.9.refs_0_.other_ref, f32[16,4096]{1,0:T(8,128)S(1)} %get-tuple-element.39.refs_1_, bf16[25,512,256]{2,1,0:T(8,128)(2,1)S(1)} %get-tuple-element.40.refs_2_, ...), custom_call_target="tpu_custom_call" | custom-call | flops 1000000000 | bytes 7200000 | tf_op jit(solution)/shard_map/pallas_call | solution.py:407
  56.1 3.8 %collective-permute-done.7.two_ref = f32[16,128]{1,0:T(8,128)S(1)} collective-permute-done((f32[16,128]{1,0:T(8,128)S(1)}, f32[16,128]{1,0:T(8,128)S(1)}, u32[]{:S(2)}, u32[]{:S(2)}) %collective-permute-start.7) | collective-permute-done | bytes 8224 | tf_op jit(solution)/shard_map/ppermute | solution.py:440
  59.9 0.0 collective-permute-done.8.second_table_ref
  59.9 0.0 collective-permute-done.10.third_ref
  59.9 3.1 %shard_map.95 = (f32[16,4096]{1,0:T(8,128)}, f32[16,4096]{1,0:T(8,128)}) custom-call(s32[16,32]{1,0:T(8,128)S(1)} %get-tuple-element.23.at_ref, f32[16,128]{1,0:T(8,128)S(1)} %shard_map.93.one_ref, f32[16,128]{1,0:T(8,128)S(1)} %collective-permute-done.7.two_ref, f32[16,1024]{1,0:T(8,128)S(1)} %collective-permute-done.8.second_table_ref, ...), custom_call_target="tpu_custom_call" | custom-call | flops 1500000000 | bytes 10800000 | tf_op jit(solution)/shard_map/pallas_call | solution.py:407
  (14 shorter events, 0.1 us)
Async XLA Ops:
  2.4 1.8 %collective-permute-start = (f32[16,5632]{1,0:T(8,128)S(1)}, f32[16,5632]{1,0:T(8,128)S(1)}, u32[]{:S(2)}, u32[]{:S(2)}) collective-permute-start(f32[16,5632]{1,0:T(8,128)S(1)} %get-tuple-element.25.refs_1_), channel_id=1, source_target_pairs={{0,1},{1,0},{2,3},{3,2},{4,5},{5,4},{6,7},{7,6},{8,9},{9,8},{10,11... | collective-permute-start | bytes 1081352 | tf_op jit(solution)/shard_map/ppermute | solution.py:440
  4.3 15.2 %collective-permute-start.2 = (f32[16,6400]{1,0:T(8,128)S(1)}, f32[16,6400]{1,0:T(8,128)S(1)}, u32[]{:S(2)}, u32[]{:S(2)}) collective-permute-start(f32[16,6400]{1,0:T(8,128)S(1)} %pad_maximum_fusion), channel_id=1, source_target_pairs={{1,2},{2,1},{3,4},{4,3},{5,6},{6,5},{7,8},{8,7},{9,10},{10,9},{11,... | collective-permute-start | bytes 1228808 | tf_op jit(solution)/shard_map/ppermute | solution.py:440
  19.5 11.1 %collective-permute-start.3 = (f32[16,2304]{1,0:T(8,128)S(1)}, f32[16,2304]{1,0:T(8,128)S(1)}, u32[]{:S(2)}, u32[]{:S(2)}) collective-permute-start(f32[16,2304]{1,0:T(8,128)S(1)} %pad_maximum_fusion.2), channel_id=1, source_target_pairs={{1,5},{2,14},{3,7},{4,0},{5,9},{6,2},{7,11},{8,4},{9,13},{10,6},{1... | collective-permute-start | bytes 442376 | tf_op jit(solution)/shard_map/ppermute | solution.py:440
  20.9 9.8 %collective-permute-start.1 = (f32[16,1536]{1,0:T(8,128)S(1)}, f32[16,1536]{1,0:T(8,128)S(1)}, u32[]{:S(2)}, u32[]{:S(2)}) collective-permute-start(f32[16,1536]{1,0:T(8,128)S(1)} %pad_maximum_fusion.3), channel_id=1, source_target_pairs={{0,13},{1,4},{2,15},{3,6},{4,1},{5,8},{6,3},{7,10},{8,5},{9,12},{1... | collective-permute-start | bytes 294920 | tf_op jit(solution)/shard_map/ppermute | solution.py:440
  35.0 1.7 %collective-permute-start.4 = (f32[16,4736]{1,0:T(8,128)S(1)}, f32[16,4736]{1,0:T(8,128)S(1)}, u32[]{:S(2)}, u32[]{:S(2)}) collective-permute-start(f32[16,4736]{1,0:T(8,128)S(1)} %get-tuple-element.35.refs_1_), channel_id=1, source_target_pairs={{0,1},{1,0},{2,3},{3,2},{4,5},{5,4},{6,7},{7,6},{8,9},{9,8},{10,11... | collective-permute-start | bytes 909320 | tf_op jit(solution)/shard_map/ppermute | solution.py:440
  36.7 12.9 %collective-permute-start.9 = (f32[16,5120]{1,0:T(8,128)S(1)}, f32[16,5120]{1,0:T(8,128)S(1)}, u32[]{:S(2)}, u32[]{:S(2)}) collective-permute-start(f32[16,5120]{1,0:T(8,128)S(1)} %pad_maximum_fusion.1), channel_id=1, source_target_pairs={{1,2},{2,1},{3,4},{4,3},{5,6},{6,5},{7,8},{8,7},{9,10},{10,9},{11,... | collective-permute-start | bytes 983048 | tf_op jit(solution)/shard_map/ppermute | solution.py:440
  42.9 6.4 %collective-permute-start.5 = (f32[16,128]{1,0:T(8,128)S(1)}, f32[16,128]{1,0:T(8,128)S(1)}, u32[]{:S(2)}, u32[]{:S(2)}) collective-permute-start(f32[16,128]{1,0:T(8,128)S(1)} %shard_map.91.one_ref), channel_id=1, source_target_pairs={{0,2},{1,3},{2,4},{3,5},{4,6},{5,7},{6,8},{7,9},{8,10},{9,11},{10,... | collective-permute-start | bytes 24584 | tf_op jit(solution)/shard_map/ppermute | solution.py:440
  45.1 14.8 %collective-permute-start.8 = (f32[16,1024]{1,0:T(8,128)S(1)}, f32[16,1024]{1,0:T(8,128)S(1)}, u32[]{:S(2)}, u32[]{:S(2)}) collective-permute-start(f32[16,1024]{1,0:T(8,128)S(1)} %pad_maximum_fusion.5), channel_id=1, source_target_pairs={{0,13},{1,4},{2,15},{3,6},{4,1},{5,8},{6,3},{7,10},{8,5},{9,12},{1... | collective-permute-start | bytes 196616 | tf_op jit(solution)/shard_map/ppermute | solution.py:440
  49.6 5.5 %collective-permute-start.6 = (f32[16,128]{1,0:T(8,128)S(1)}, f32[16,128]{1,0:T(8,128)S(1)}, u32[]{:S(2)}, u32[]{:S(2)}) collective-permute-start(f32[16,128]{1,0:T(8,128)S(1)} %shard_map.92.one_ref), channel_id=1, source_target_pairs={{0,4},{1,5},{2,6},{3,7},{4,8},{5,9},{6,10},{7,11},{8,12},{9,13},{1... | collective-permute-start | bytes 24584 | tf_op jit(solution)/shard_map/ppermute | solution.py:440
  49.6 10.3 %collective-permute-start.10 = (f32[16,1536]{1,0:T(8,128)S(1)}, f32[16,1536]{1,0:T(8,128)S(1)}, u32[]{:S(2)}, u32[]{:S(2)}) collective-permute-start(f32[16,1536]{1,0:T(8,128)S(1)} %pad_maximum_fusion.4), channel_id=1, source_target_pairs={{1,5},{2,14},{3,7},{4,0},{5,9},{6,2},{7,11},{8,4},{9,13},{10,6},{1... | collective-permute-start | bytes 294920 | tf_op jit(solution)/shard_map/ppermute | solution.py:440
  55.4 4.6 %collective-permute-start.7 = (f32[16,128]{1,0:T(8,128)S(1)}, f32[16,128]{1,0:T(8,128)S(1)}, u32[]{:S(2)}, u32[]{:S(2)}) collective-permute-start(f32[16,128]{1,0:T(8,128)S(1)} %shard_map.93.one_ref), channel_id=1, source_target_pairs={{0,8},{1,9},{2,10},{3,11},{4,12},{5,13},{6,14},{7,15},{8,0},{9,1},... | collective-permute-start | bytes 24584 | tf_op jit(solution)/shard_map/ppermute | solution.py:440
where the time goes:
time: 62.7 us; the launch traced here: 63.1 us
  Pallas kernels  31.5 us (50%)
  waiting for transfers between devices  19.3 us (31%)
  starting transfers between devices  11.4 us (18%)
  between operations  0.8 us (1%)
    pallas_call x10, Pallas kernels, call(): pl.pallas_call(kernel, out_shape=[pltpu.VMEM(*out) if m == 'p' else jax.S...  31.5 us
    ppermute x11, waiting for transfers between devices, move(): return lax.ppermute(value, 'clus', pairs)  19.3 us
    ppermute x11, starting transfers between devices, move(): return lax.ppermute(value, 'clus', pairs)  11.4 us
  transfers between devices with their start and end apart: 11, of which 6 were waited for; matrix products, arithmetic and copies ran while one was open for 0% of the time, Pallas kernels for 35%

commit v1 on v0

--- a/solution.py
+++ b/solution.py
@@ -66,8 +66,8 @@
 
 def pair_list(near, position, clusters):
     block = lax.div(near, clusters) - position
-    place = (1 - block * (1 - 2 * lax.rem(position, 2))) * clusters + lax.rem(near, clusters)
-    place = place.astype(F32)
+    partner = block * (1 - 2 * lax.rem(position, 2)) > 0
+    place = (lax.rem(near, clusters) + jnp.where((block != 0) & ~partner, clusters, 0)).astype(F32)
     across = lax.broadcasted_iota(jnp.int32, (clusters, clusters), 1)
     down = lax.broadcasted_iota(jnp.int32, (clusters, clusters), 0)
     upright = lambda value: jnp.sum(jnp.where(across == down, value, 0.0), axis=1, keepdims=True)
@@ -76,7 +76,7 @@
     rows = lax.broadcasted_iota(jnp.int32, (8, LANES), 0)
     out = jnp.zeros((8, LANES), F32)
     for which in range(2):
-        here = place >= 2.0 * clusters if which else place < 2.0 * clusters
+        here = block != 0 if which else block == 0
         live = jnp.where(here & (near >= 0), 1.0, 0.0)
         counts = sum(live[k:k + 1] for k in range(near.shape[0]))
         first = jnp.sum(jnp.where(across < down, counts, 0.0), axis=1, keepdims=True)
@@ -84,20 +84,20 @@
         for k in range(near.shape[0]):
             alive = upright(live[k:k + 1])
             hit = jnp.where(row == first, alive, 0.0)
-            found = found + hit * (target * 64 + upright(place[k:k + 1]) - 2.0 * clusters * which)
+            found = found + hit * (target * 64 + upright(place[k:k + 1]))
             first = first + alive
         count = jnp.sum(counts, axis=1, keepdims=True)
-        found = jnp.where(row[0:1] < count, jnp.sum(found, axis=0, keepdims=True), (2.0 - which) * clusters)
+        found = jnp.where(row[0:1] < count, jnp.sum(found, axis=0, keepdims=True), (1.0 + which) * clusters)
         out = jnp.where(rows == which, found, jnp.where(rows == 2 + which, count, out))
     return out.astype(jnp.int32)
 
 
-def prepare_kernel(cl, vcl, rank, position_ref, vertices_hbm, corners_hbm, krylov_hbm, basis_hbm, far_hbm, near_hbm, offsets_hbm,
-                   payload_ref, area_ref, center_ref, at_ref, pairs_ref, basis_ref, krylov_ref, offsets_ref,
+def prepare_kernel(cl, vcl, rank, position_ref, vertices_hbm, corners_hbm, krylov_hbm, basis_hbm, far_hbm, near_hbm, offsets_hbm, weights_hbm,
+                   payload_ref, area_ref, center_ref, at_ref, pairs_ref, basis_ref, krylov_ref, offsets_ref, weights_ref,
                    vertices_ref, corners_ref, raw_ref, far_ref, near_ref, mesh_ref, local_ref, sems):
     moves = copies((
         (vertices_hbm, vertices_ref), (corners_hbm, corners_ref), (krylov_hbm, krylov_ref), (basis_hbm, raw_ref),
-        (far_hbm, far_ref), (near_hbm, near_ref), (offsets_hbm, offsets_ref),
+        (far_hbm, far_ref), (near_hbm, near_ref), (offsets_hbm, offsets_ref), (weights_hbm.at[position_ref[0]], weights_ref),
     ), sems)
     rhs, panels = krylov_ref.shape
     clusters = panels // cl
@@ -151,6 +151,7 @@
     moves[5].wait()
     pairs_ref[...] = pair_list(near_ref[...], position_ref[0], clusters)
     moves[6].wait()
+    moves[7].wait()
 
 
 def columns_of(payload_ref, panels, c, cl, columns_ref, at):
@@ -191,8 +192,8 @@
     if which:
         columns_ref, start_ref, even_ref, odd_ref, near_out_ref, pieces_ref, sources_ref, total_ref = refs[number:]
     else:
-        even_ref, odd_ref, near_out_ref, columns_ref, tail_ref, pieces_ref, sources_ref, total_ref = refs[number:]
-        tail_ref[...] = blocks[1][:, blocks[1].shape[1] - tail_ref.shape[1]:]
+        _, even_ref, odd_ref, near_out_ref, columns_ref, tail_ref, pieces_ref, sources_ref, total_ref = refs[number:]
+        tail_ref[...] = blocks[0][:, blocks[0].shape[1] - tail_ref.shape[1]:]
     panels = near_out_ref.shape[1]
     clusters = panels // cl
     steps = (pairs_ref[2 + which, 0] + 1) // 2
@@ -204,7 +205,7 @@
     fill_charges(pieces_ref, blocks, clusters, cl)
     for c in range(clusters):
         if not which:
-            columns_of(blocks[1], panels, c, cl, columns_ref, c)
+            columns_of(blocks[0], panels, c, cl, columns_ref, c)
         total_ref[c] = jnp.zeros_like(total_ref[c])
     odd_ref[0] = jnp.zeros_like(odd_ref[0])
 
@@ -243,8 +244,8 @@
     if which:
         start_ref, even_ref, odd_ref, near_out_ref, pieces_ref, total_ref = refs[number:]
     else:
-        even_ref, odd_ref, near_out_ref, tail_ref, pieces_ref, total_ref = refs[number:]
-        tail_ref[...] = blocks[1][:, blocks[1].shape[1] - tail_ref.shape[1]:]
+        _, even_ref, odd_ref, near_out_ref, tail_ref, pieces_ref, total_ref = refs[number:]
+        tail_ref[...] = blocks[0][:, blocks[0].shape[1] - tail_ref.shape[1]:]
     clusters = near_out_ref.shape[1] // cl
     fill_charges(pieces_ref, blocks, clusters, cl)
     for c in range(clusters):
@@ -287,7 +288,11 @@
 
 
 def six_tables(width, second_ref, other_ref, third_ref):
-    return (second_ref, width), (second_ref, 0), (other_ref, other_ref.shape[1] - width), (third_ref, 2 * width), (third_ref, width), (third_ref, 0)
+    gap = third_ref.shape[1] - 3 * width
+    return (
+        (second_ref, width), (second_ref, 0), (other_ref, other_ref.shape[1] - width),
+        (third_ref, 2 * width + gap), (third_ref, width + gap), (third_ref, 0),
+    )
 
 
 def pick(source_ref, at_ref, c, g, per, lane):
@@ -347,30 +352,38 @@
     payload_ref[:, panels + span:] = in_lanes(squared, correlation, jnp.sum(residual * residual, axis=1, keepdims=True), local)
 
 
-def finish_kernel(cl, rank, total, at_ref, one_ref, two_ref, second_table_ref, other_ref, third_ref, near_ref, area_ref, image_ref, coupling_ref, basis_ref, krylov_ref,
-                  next_hbm, second_hbm, pieces_ref, gathered_ref, fields_ref, next_ref, second_ref, sems):
+def far_again_kernel(cl, rank, at_ref, second_ref, other_ref, third_ref, near_ref, area_ref, coupling_ref, basis_ref,
+                     image_ref, pieces_ref, gathered_ref, fields_ref):
     clusters = near_ref.shape[1] // cl
     per = LANES // rank
+    load_window(six_tables(clusters * rank + LANES, second_ref, other_ref, third_ref), clusters, rank, pieces_ref, None)
+    lane = lax.broadcasted_iota(jnp.int32, (1, LANES), 1) // rank
+    for c in range(clusters):
+        for g in range(at_ref.shape[1] // per):
+            gathered_ref[c, :, g * LANES:(g + 1) * LANES] = pick(pieces_ref, at_ref, c, g, per, lane)
+    far_fields(gathered_ref, coupling_ref, fields_ref)
+    for c in range(clusters):
+        lanes = slice(c * cl, (c + 1) * cl)
+        image_ref[:, lanes] = COULOMB * area_ref[c:c + 1, :] * (near_ref[:, lanes] + far_potential(fields_ref, c, basis_ref[:, lanes]))
+
+
+def finish_kernel(total, one_ref, two_ref, image_ref, again_ref, krylov_ref, next_hbm, second_hbm, next_ref, second_ref, sems):
     squared, correlation, energy, local = merged([one_ref[...], two_ref[...]])
     projection = correlation / (squared + 1e-06)
     gap = projection - local
     scaling = 1.0 / jnp.sqrt((energy + gap * gap * squared) / total + 1e-06)
-    next_ref[...] = (image_ref[...] - projection * krylov_ref[...]) * scaling
-    moves = copies(((next_ref, next_hbm),), sems)
-    load_window(six_tables(clusters * rank, second_table_ref, other_ref, third_ref), clusters, rank, pieces_ref, None)
-    lane = lax.broadcasted_iota(jnp.int32, (1, LANES), 1) // rank
-    for c in range(clusters):
-        for g in range(at_ref.shape[1] // per):
-            gathered_ref[c, :, g * LANES:(g + 1) * LANES] = pick(pieces_ref, at_ref, c, g, per, lane)
-    far_fields(gathered_ref, coupling_ref, fields_ref)
-    for c in range(clusters):
-        lanes = slice(c * cl, (c + 1) * cl)
-        image = COULOMB * area_ref[c:c + 1, :] * (near_ref[:, lanes] + far_potential(fields_ref, c, basis_ref[:, lanes]))
-        second_ref[:, lanes] = (image - projection * image_ref[:, lanes]) * scaling
-    moves.append(pltpu.make_async_copy(second_ref, second_hbm, sems.at[1]))
-    moves[1].start()
-    moves[0].wait()
-    moves[1].wait()
+    moves = []
+    half = next_ref.shape[1] // 2
+    for h in range(2):
+        lanes = slice(h * half, (h + 1) * half)
+        image = image_ref[:, lanes]
+        next_ref[:, lanes] = (image - projection * krylov_ref[:, lanes]) * scaling
+        second_ref[:, lanes] = (again_ref[:, lanes] - projection * image) * scaling
+        for held, hbm in ((next_ref, next_hbm), (second_ref, second_hbm)):
+            moves.append(pltpu.make_async_copy(held.at[:, lanes], hbm.at[:, lanes], sems.at[len(moves)]))
+            moves[-1].start()
+    for move in moves:
+        move.wait()
 
 
 def ratio(correlation, squared):
@@ -385,15 +398,61 @@
     return out
 
 
-def merged(groups):
-    squared = sum(group[:, 0:1] for group in groups)
-    correlation = sum(group[:, 1:2] for group in groups)
+def merged(groups, weights=None):
+    weights = weights or [1.0] * len(groups)
+    squared = sum(weight * group[:, 0:1] for group, weight in zip(groups, weights))
+    correlation = sum(weight * group[:, 1:2] for group, weight in zip(groups, weights))
     local = ratio(correlation, squared)
     energy = 0.0
-    for group in groups:
+    for group, weight in zip(groups, weights):
         gap = local - group[:, 3:4]
-        energy = energy + (group[:, 2:3] + gap * gap * group[:, 0:1])
+        energy = energy + weight * (group[:, 2:3] + gap * gap * group[:, 0:1])
     return squared, correlation, energy, local
+
+
+def known_sums(tail_ref, partner_ref, other_ref, second_ref, third_ref):
+    width = tail_ref.shape[1]
+    ends = [(tail_ref, width), (partner_ref, partner_ref.shape[1]), (other_ref, other_ref.shape[1] - width), (other_ref, other_ref.shape[1])]
+    ends += [(second_ref, width), (second_ref, 2 * width)]
+    ends += [(third_ref, width), (third_ref, width + LANES), (third_ref, 2 * width + LANES), (third_ref, 3 * width + LANES)]
+    return [ref[:, end - LANES:end] for ref, end in ends]
+
+
+def known_sums_kernel(weights_ref, *refs):
+    groups = known_sums(*refs[:5])
+    for side, out_ref in enumerate(refs[5:]):
+        weights = [weights_ref[0:1, 16 * side + i:16 * side + i + 1] for i in range(len(groups))]
+        out_ref[...] = in_lanes(*merged(groups, weights))
+
+
+def completing(devices, *moves):
+    partner, other, second, third = ({target: source for source, target in move} for move in moves)
+    slots = []
+    for i in range(devices):
+        two, three = second[i], third[i]
+        slots.append([i, partner[i], other[i], partner[other[i]], two, partner[two], three, partner[three], other[three], partner[other[three]]])
+    known = [set(slot) for slot in slots]
+    everyone = set(range(devices))
+    target_of = {}
+
+    def matched(target, seen):
+        for source in range(devices):
+            if source not in seen and known[target] | known[source] == everyone:
+                seen.add(source)
+                if source not in target_of or matched(target_of[source], seen):
+                    target_of[source] = target
+                    return True
+        return False
+
+    if not all(matched(i, set()) for i in range(devices)):
+        return None
+    weights = np.zeros((devices, 8, LANES), np.float32)
+    for i in range(devices):
+        for at, device in enumerate(slots[i]):
+            if device not in slots[i][:at]:
+                weights[i, :, at] = 1.0
+                weights[i, :, 16 + at] = device not in known[target_of[i]]
+    return sorted(target_of.items()), weights
 
 
 def merge_kernel(one_ref, two_ref, out_ref):
@@ -436,6 +495,9 @@
     third = [(i, i + 4 * (2 * (i % 2) - 1)) for i in range(1, devices - 1)] + [(0, 3), (devices - 1, devices - 4)]
     third = [(i, j % devices) for i, j in third]
 
+    completion = completing(devices, pairing, bridging, second, third)
+    weights = completion[1] if completion else np.zeros((devices, 8, LANES), np.float32)
+
     def move(value, pairs):
         return lax.ppermute(value, "clus", pairs)
 
@@ -446,15 +508,16 @@
         other = move(jnp.concatenate([value[:, :first], pair], axis=1), bridging)
         return partner, other, move(pair, second)
 
-    def last_exchange(tail, other, width):
-        return move(jnp.concatenate([tail[:, :width], other[:, other.shape[1] - 2 * width:]], axis=1), third)
+    def last_exchange(tail, between, other):
+        pair = other[:, other.shape[1] - 2 * tail.shape[1]:]
+        return move(jnp.concatenate([tail, *between, pair], axis=1), third)
 
     whole = ((rhs, panels), F32)
-    payload, area, centers, at, pairs, basis, krylov, offsets = call(
+    payload, area, centers, at, pairs, basis, krylov, offsets, weights = call(
         functools.partial(prepare_kernel, cl, vcl, rank),
         [
             ((rhs, panels + 3 * cl + width), F32), ((clusters, cl), F32), ((clusters, 3 * LANES), F32),
-            (far_pairs.shape, jnp.int32), ((8, LANES), jnp.int32), ((2 * rank, panels), BF16), whole, (offsets.shape, F32),
+            (far_pairs.shape, jnp.int32), ((8, LANES), jnp.int32), ((2 * rank, panels), BF16), whole, (offsets.shape, F32), ((8, LANES), F32),
         ],
         [
             pltpu.VMEM(vertices.shape, F32),
@@ -464,10 +527,10 @@
             pltpu.VMEM((slots, clusters), jnp.int32),
             pltpu.VMEM((3 * clusters, vcl), F32),
             pltpu.VMEM((3 * panels // LANES, LANES), jnp.int32),
-            pltpu.SemaphoreType.DMA((7,)),
+            pltpu.SemaphoreType.DMA((8,)),
         ],
-        "shhhhhhh>vvvvvppp",
-        position, vertices, panel_vertices, krylov, basis, far_pairs, near_pairs.T, offsets,
+        "shhhhhhhh>vvvvvpppp",
+        position, vertices, panel_vertices, krylov, basis, far_pairs, near_pairs.T, offsets, jnp.asarray(weights),
         us=1.5,
     )
     partner, other, two = exchange(payload, panels + 3 * cl, width)
@@ -483,21 +546,21 @@
         return pltpu.VMEM((number * clusters + 1, 8, cl), F32)
 
     even, odd, near, columns, tail = call(
-        functools.partial(near_kernel, cl, 0, 2),
+        functools.partial(near_kernel, cl, 0, 1),
         [*kept(clusters * slots), whole, ((clusters, 3, cl, LANES), F32), ((rhs, width), F32)],
+        [pieces(1), sources(1), total],
+        "svv>ppvpv",
+        pairs, payload, partner,
+        us=6.0,
+    )
+    three = last_exchange(tail, [], other)
+    even_other, odd_other, near = call(
+        functools.partial(near_kernel, cl, 1, 2),
+        [*kept(clusters * (slots - 1)), whole],
         [pieces(2), sources(2), total],
-        "svv>ppvpv",
-        pairs, partner, payload,
-        us=8.0,
-    )
-    three = last_exchange(tail, other, width)
-    even_other, odd_other, near = call(
-        functools.partial(near_kernel, cl, 1, 1),
-        [*kept(clusters * (slots - 1)), whole],
-        [pieces(1), sources(1), total],
-        "svpv>ppv",
-        pairs, other, columns, near,
-        us=3.0,
+        "svvpv>ppv",
+        pairs, partner, other, columns, near,
+        us=4.0,
     )
     tiles = 6 * per * span // LANES
     window = pltpu.VMEM((tiles, 2 * rhs, LANES), BF16)
@@ -511,38 +574,49 @@
         at, two, other, three, centers, area, near, basis, krylov, offsets,
         us=4.5,
     )
-    partner, other, two = exchange(payload, panels, span)
-    near, one = call(
-        functools.partial(near_again_kernel, cl, 0, 2),
+    partner, other, two = exchange(payload, panels, span + LANES)
+    near, tail = call(
+        functools.partial(near_again_kernel, cl, 0, 1),
         [whole, ((rhs, span + LANES), F32)],
+        [pieces(1), total],
+        "svvpp>vv",
+        pairs, payload, partner, even, odd,
+        us=2.5,
+    )
+    three = last_exchange(tail, [partner[:, panels + span:]], other)
+    (near,) = call(
+        functools.partial(near_again_kernel, cl, 1, 2),
+        [whole],
         [pieces(2), total],
-        "svvpp>vv",
-        pairs, partner, payload, even, odd,
-        us=2.5,
-    )
-    three = last_exchange(one, other, span)
-    many = partner
-    size = 2
-    while size < devices:
-        (one,) = call(merge_kernel, [((rhs, LANES), F32)], [], "vv>v", one, many, us=0.3)
-        many = move(one, [(i, (i + size) % devices) for i in range(devices)])
-        size = 2 * size
-    (near,) = call(
-        functools.partial(near_again_kernel, cl, 1, 1),
+        "svvvpp>v",
+        pairs, partner, other, near, even_other, odd_other,
+        us=2.0,
+    )
+    sums_shape = ((rhs, LANES), F32)
+    if completion:
+        one, many = call(known_sums_kernel, [sums_shape] * 2, [], "pvvvvv>vv", weights, tail, partner, other, two, three, us=0.3)
+        many = move(many, completion[0])
+    else:
+        one, many, size = tail, partner, 2
+        while size < devices:
+            (one,) = call(merge_kernel, [sums_shape], [], "vv>v", one, many, us=0.3)
+            many = move(one, [(i, (i + size) % devices) for i in range(devices)])
+            size = 2 * size
+    (again,) = call(
+        functools.partial(far_again_kernel, cl, rank),
         [whole],
-        [pieces(1), total],
-        "svvpp>v",
-        pairs, other, near, even_other, odd_other,
+        [window, gathered, fields],
+        "svvvvvpp>v",
+        at, two, other, three, near, area, coupling, basis,
         us=2.0,
     )
     here = pltpu.VMEM((rhs, panels), F32)
     return tuple(call(
-        functools.partial(finish_kernel, cl, rank, panels * devices),
+        functools.partial(finish_kernel, panels * devices),
         [whole, whole],
-        [window, gathered, fields, here, here, pltpu.SemaphoreType.DMA((2,))],
-        "svvvvvvvvppp>hh",
-        at, one, many, two, other, three, near, area, image, coupling, basis, krylov,
-        us=3.0,
+        [here, here, pltpu.SemaphoreType.DMA((4,))],
+        "vvvvp>hh",
+        one, many, image, again, krylov,
     ))
 
 

time: 62.7 us -> 59.6 us (0.951); the launches traced: 63.1 us -> 59.1 us
  starting transfers between devices: 11.4 us -> 24.2 us
  waiting for transfers between devices: 19.3 us -> 10 us
  Pallas kernels: 31.5 us -> 24 us
    ppermute x11 -> x9, starting transfers between devices: 11.4 us -> 24.2 us  [move(): return lax.ppermute(value, 'clus', pairs)]
    ppermute x11 -> x9, waiting for transfers between devices: 19.3 us -> 10 us  [move(): return lax.ppermute(value, 'clus', pairs)]
    pallas_call x10 -> x9, Pallas kernels: 31.5 us -> 24 us  [call(): pl.pallas_call(kernel, out_shape=[pltpu.VMEM(*out) if m == 'p' else jax.S...]
  transfers between devices with their start and end apart: 11 -> 9, of which waited for: 6 -> 4; matrix products, arithmetic and copies ran while one was open for 0% -> 0% of each run, Pallas kernels for 35% -> 27%
where the time goes in v1:
time: 59.6 us; the launch traced here: 59.1 us
  starting transfers between devices  24.2 us (41%)
  Pallas kernels  24 us (40%)
  waiting for transfers between devices  10 us (17%)
  between operations  0.81 us (1%)
    ppermute x9, starting transfers between devices, move(): return lax.ppermute(value, 'clus', pairs)  24.2 us
    pallas_call x9, Pallas kernels, call(): pl.pallas_call(kernel, out_shape=[pltpu.VMEM(*out) if m == 'p' else jax.S...  24 us
    ppermute x9, waiting for transfers between devices, move(): return lax.ppermute(value, 'clus', pairs)  10 us
  transfers between devices with their start and end apart: 9, of which 4 were waited for; matrix products, arithmetic and copies ran while one was open for 0% of the time, Pallas kernels for 27%

profile of v1, /device:TPU:0, one launch (start us, length us, event | category | flops | bytes accessed | tf_op | source)
XLA Modules:
  0.0 59.1 jit_solution(5102869531874374358)
XLA Ops:
  0.6 1.8 %shard_map.95 = (f32[16,5632]{1,0:T(8,128)S(1)}, f32[16,256]{1,0:T(8,128)S(1)}, f32[16,384]{1,0:T(8,128)S(1)}, s32[16,32]{1,0:T(8,128)S(1)}, s32[8,128]{1,0:T(8,...) custom-call(s32[1]{0:T(128)} %bitcast.position_ref, ...), custom_call_target="tpu_custom_call" | custom-call | flops 750000000 | bytes 5400000 | tf_op jit(solution)/shard_map/pallas_call | solution.py:466
  2.5 0.5 collective-permute-start
  3.0 1.3 %collective-permute-done.refs_1_.refs_0_ = f32[16,5632]{1,0:T(8,128)S(1)} collective-permute-done((f32[16,5632]{1,0:T(8,128)S(1)}, f32[16,5632]{1,0:T(8,128)S(1)}, u32[]{:S(2)}, u32[]{:S(2)}) %collective-permute-start) | collective-permute-done | bytes 360480 | tf_op jit(solution)/shard_map/ppermute | solution.py:502
  4.3 0.7 %collective-permute-start.2 = (f32[16,6400]{1,0:T(8,128)S(1)}, f32[16,6400]{1,0:T(8,128)S(1)}, u32[]{:S(2)}, u32[]{:S(2)}) collective-permute-start(f32[16,6400]{1,0:T(8,128)S(1)} %pad_maximum_fusion), channel_id=1, source_target_pairs={{1,2},{2,1},{3,4},{4,3},{5,6},{6,5},{7,8},{8,7},{9,10},{10,9},{11,... | collective-permute-start | bytes 1228808 | tf_op jit(solution)/shard_map/ppermute | solution.py:502
  5.0 7.5 %collective-permute-start.1 = (f32[16,1536]{1,0:T(8,128)S(1)}, f32[16,1536]{1,0:T(8,128)S(1)}, u32[]{:S(2)}, u32[]{:S(2)}) collective-permute-start(f32[16,1536]{1,0:T(8,128)S(1)} %pad_maximum_fusion.4), channel_id=1, source_target_pairs={{0,13},{1,4},{2,15},{3,6},{4,1},{5,8},{6,3},{7,10},{8,5},{9,12},{1... | collective-permute-start | bytes 294920 | tf_op jit(solution)/shard_map/ppermute | solution.py:502
  12.5 7.8 %shard_map.96 = (bf16[33,512,256]{2,1,0:T(8,128)(2,1)S(1)}, bf16[33,512,256]{2,1,0:T(8,128)(2,1)S(1)}, f32[16,4096]{1,0:T(8,128)S(1)}, f32[16,3,256,128]{3,2,1,0:T(8,128)S(1)}, f32[16,768]{1,0:T(8,128)S(1)}) custom-call(s32[8,128]{1,0:T(8,128)S(1)} %get-tuple-element.27.pairs_ref, f32[16,5632]{1,0:T(8,128)S(1)} %get-tuple-element.29.refs_0_, ...), custom_call_target="tpu_custom_call" | custom-call | flops 3000000000 | bytes 21600000 | tf_op jit(solution)/shard_map/pallas_call | solution.py:466
  20.4 0.0 collective-permute-done.2.refs_1_.other_ref
  20.4 0.1 collective-permute-start.3
  20.5 2.0 %shard_map.97 = (bf16[25,512,256]{2,1,0:T(8,128)(2,1)S(1)}, bf16[25,512,256]{2,1,0:T(8,128)(2,1)S(1)}, f32[16,4096]{1,0:T(8,128)S(1)}) custom-call(s32[8,128]{1,0:T(8,128)S(1)} %get-tuple-element.27.pairs_ref, f32[16,5632]{1,0:T(8,128)S(1)} %collective-permute-done.refs_1_.refs_0_, f32[16,6400]{1,0:T(8,128)S(1)} %collective-permute-done.2.refs_1_.other_ref, ...), custom_call_target="tpu_custom_call" | custom-call | flops 2000000000 | bytes 14400000 | tf_op jit(solution)/shard_map/pallas_call | solution.py:466
  22.5 0.0 collective-permute-done.1.second_ref
  22.5 4.7 %collective-permute-done.3.third_ref = f32[16,2304]{1,0:T(8,128)S(1)} collective-permute-done((f32[16,2304]{1,0:T(8,128)S(1)}, f32[16,2304]{1,0:T(8,128)S(1)}, u32[]{:S(2)}, u32[]{:S(2)}) %collective-permute-start.3) | collective-permute-done | bytes 147488 | tf_op jit(solution)/shard_map/ppermute | solution.py:502
  27.2 4.3 %shard_map.98 = (f32[16,4096]{1,0:T(8,128)S(1)}, f32[16,4736]{1,0:T(8,128)S(1)}, bf16[16,64,1024]{2,1,0:T(8,128)(2,1)S(1)}) custom-call(s32[16,32]{1,0:T(8,128)S(1)} %get-tuple-element.28.at_ref, f32[16,1536]{1,0:T(8,128)S(1)} %collective-permute-done.1.second_ref, f32[16,6400]{1,0:T(8,128)S(1)} %collective-permute-done.2.refs_1_.other_ref, ...), custom_call_target="tpu_custom_call" | custom-call | flops 2249999872 | bytes 16200000 | tf_op jit(solution)/shard_map/pallas_call | solution.py:466
  31.5 0.1 collective-permute-start.4
  31.6 1.6 %collective-permute-done.4.refs_1_.refs_0_ = f32[16,4736]{1,0:T(8,128)S(1)} collective-permute-done((f32[16,4736]{1,0:T(8,128)S(1)}, f32[16,4736]{1,0:T(8,128)S(1)}, u32[]{:S(2)}, u32[]{:S(2)}) %collective-permute-start.4) | collective-permute-done | bytes 303136 | tf_op jit(solution)/shard_map/ppermute | solution.py:502
  33.2 0.7 %collective-permute-start.5 = (f32[16,5376]{1,0:T(8,128)S(1)}, f32[16,5376]{1,0:T(8,128)S(1)}, u32[]{:S(2)}, u32[]{:S(2)}) collective-permute-start(f32[16,5376]{1,0:T(8,128)S(1)} %pad_maximum_fusion.1), channel_id=1, source_target_pairs={{1,2},{2,1},{3,4},{4,3},{5,6},{6,5},{7,8},{8,7},{9,10},{10,9},{11,... | collective-permute-start | bytes 1032200 | tf_op jit(solution)/shard_map/ppermute | solution.py:502
  33.9 2.8 %shard_map.99 = (f32[16,4096]{1,0:T(8,128)S(1)}, f32[16,640]{1,0:T(8,128)S(1)}) custom-call(s32[8,128]{1,0:T(8,128)S(1)} %get-tuple-element.27.pairs_ref, f32[16,4736]{1,0:T(8,128)S(1)} %get-tuple-element.39.refs_0_, f32[16,4736]{1,0:T(8,128)S(1)} %collective-permute-done.4.refs_1_.refs_0_, bf16[33,512,256]{2,1,0:T(8,128)(2,1)S(1)} %get-tuple-element.40.refs_2_, ...), custom_call_target="tpu_custom_call" | custom-call | flops 1250000000 | bytes 9000000 | tf_op jit(solution)/shard_map/pallas_call | solution.py:466
  36.7 0.0 collective-permute-done.5.refs_2_.refs_1_.other_ref
  36.7 6.8 %collective-permute-start.7 = (f32[16,2048]{1,0:T(8,128)S(1)}, f32[16,2048]{1,0:T(8,128)S(1)}, u32[]{:S(2)}, u32[]{:S(2)}) collective-permute-start(f32[16,2048]{1,0:T(8,128)S(1)} %pad_maximum_fusion.3), channel_id=1, source_target_pairs={{1,5},{2,14},{3,7},{4,0},{5,9},{6,2},{7,11},{8,4},{9,13},{10,6},{1... | collective-permute-start | bytes 393224 | tf_op jit(solution)/shard_map/ppermute | solution.py:502
  43.5 4.1 %collective-permute-start.6 = (f32[16,1280]{1,0:T(8,128)S(1)}, f32[16,1280]{1,0:T(8,128)S(1)}, u32[]{:S(2)}, u32[]{:S(2)}) collective-permute-start(f32[16,1280]{1,0:T(8,128)S(1)} %pad_maximum_fusion.5), channel_id=1, source_target_pairs={{0,13},{1,4},{2,15},{3,6},{4,1},{5,8},{6,3},{7,10},{8,5},{9,12},{1... | collective-permute-start | bytes 245768 | tf_op jit(solution)/shard_map/ppermute | solution.py:502
  47.5 1.2 %shard_map.101.near_ref = f32[16,4096]{1,0:T(8,128)S(1)} custom-call(s32[8,128]{1,0:T(8,128)S(1)} %get-tuple-element.27.pairs_ref, f32[16,4736]{1,0:T(8,128)S(1)} %collective-permute-done.4.refs_1_.refs_0_, f32[16,5376]{1,0:T(8,128)S(1)} %collective-permute-done.5.refs_2_.refs_1_.other_ref, f32[16,4096]{1,0:T(8,128)S(1)} %get-tuple-element.46.refs_2_, ...), custom_call_target="tpu_custom_call" | custom-call | flops 1000000000 | bytes 7200000 | tf_op jit(solution)/shard_map/pallas_call | solution.py:466
  48.7 2.4 %collective-permute-done.6.refs_3_.second_ref = f32[16,1280]{1,0:T(8,128)S(1)} collective-permute-done((f32[16,1280]{1,0:T(8,128)S(1)}, f32[16,1280]{1,0:T(8,128)S(1)}, u32[]{:S(2)}, u32[]{:S(2)}) %collective-permute-start.6) | collective-permute-done | bytes 81952 | tf_op jit(solution)/shard_map/ppermute | solution.py:502
  51.2 0.0 collective-permute-done.7.refs_4_.third_ref
  51.2 0.7 %shard_map.100 = (f32[16,128]{1,0:T(8,128)S(1)}, f32[16,128]{1,0:T(8,128)S(1)}) custom-call(f32[8,128]{1,0:T(8,128)S(1)} %get-tuple-element.26.weights_ref, f32[16,640]{1,0:T(8,128)S(1)} %get-tuple-element.42.refs_0_, f32[16,4736]{1,0:T(8,128)S(1)} %collective-permute-done.4.refs_1_.refs_0_, f32[16,5376]{1,0:T(8,128)S(1)} %collective-permute-done.5.refs_2_.refs_1_.other_ref, ...), custom_call_target="tpu_custom_call" | custom-call | flops 150000000 | bytes 1080000 | tf_op jit(solution)/shard_map/pallas_call | solution.py:466
  51.9 3.8 %collective-permute-start.8 = (f32[16,128]{1,0:T(8,128)S(1)}, f32[16,128]{1,0:T(8,128)S(1)}, u32[]{:S(2)}, u32[]{:S(2)}) collective-permute-start(f32[16,128]{1,0:T(8,128)S(1)} %get-tuple-element.44), channel_id=1, source_target_pairs={{0,11},{1,9},{2,8},{3,12},{4,15},{5,10},{6,14},{7,13},{8,1},{9,2},... | collective-permute-start | bytes 24584 | tf_op jit(solution)/shard_map/ppermute | solution.py:502
  55.7 2.2 %shard_map.102.again_ref = f32[16,4096]{1,0:T(8,128)S(1)} custom-call(s32[16,32]{1,0:T(8,128)S(1)} %get-tuple-element.28.at_ref, f32[16,1280]{1,0:T(8,128)S(1)} %collective-permute-done.6.refs_3_.second_ref, f32[16,5376]{1,0:T(8,128)S(1)} %collective-permute-done.5.refs_2_.refs_1_.other_ref, f32[16,2048]{1,0:T(8,128)S(1)} %collective-permute-done.7.refs_4_.third_ref, ...), custom_call_target="tpu_custom_call" | custom-call | flops 1000000000 | bytes 7200000 | tf_op jit(solution)/shard_map/pallas_call | solution.py:466
  57.9 0.0 collective-permute-done.8.two_ref
  57.9 1.2 %shard_map.103 = (f32[16,4096]{1,0:T(8,128)}, f32[16,4096]{1,0:T(8,128)}) custom-call(f32[16,128]{1,0:T(8,128)S(1)} %get-tuple-element.43.one_ref, f32[16,128]{1,0:T(8,128)S(1)} %collective-permute-done.8.two_ref, f32[16,4096]{1,0:T(8,128)S(1)} %get-tuple-element.45.image_ref, f32[16,4096]{1,0:T(8,128)S(1)} %shard_map.102.again_ref, ...), custom_call_target="tpu_custom_call" | custom-call | flops 500000000 | bytes 3600000 | tf_op jit(solution)/shard_map/pallas_call | solution.py:466
  (13 shorter events, 0.1 us)
Async XLA Ops:
  2.5 1.8 %collective-permute-start = (f32[16,5632]{1,0:T(8,128)S(1)}, f32[16,5632]{1,0:T(8,128)S(1)}, u32[]{:S(2)}, u32[]{:S(2)}) collective-permute-start(f32[16,5632]{1,0:T(8,128)S(1)} %get-tuple-element.29.refs_0_), channel_id=1, source_target_pairs={{0,1},{1,0},{2,3},{3,2},{4,5},{5,4},{6,7},{7,6},{8,9},{9,8},{10,11... | collective-permute-start | bytes 1081352 | tf_op jit(solution)/shard_map/ppermute | solution.py:502
  4.3 16.1 %collective-permute-start.2 = (f32[16,6400]{1,0:T(8,128)S(1)}, f32[16,6400]{1,0:T(8,128)S(1)}, u32[]{:S(2)}, u32[]{:S(2)}) collective-permute-start(f32[16,6400]{1,0:T(8,128)S(1)} %pad_maximum_fusion), channel_id=1, source_target_pairs={{1,2},{2,1},{3,4},{4,3},{5,6},{6,5},{7,8},{8,7},{9,10},{10,9},{11,... | collective-permute-start | bytes 1228808 | tf_op jit(solution)/shard_map/ppermute | solution.py:502
  5.0 17.5 %collective-permute-start.1 = (f32[16,1536]{1,0:T(8,128)S(1)}, f32[16,1536]{1,0:T(8,128)S(1)}, u32[]{:S(2)}, u32[]{:S(2)}) collective-permute-start(f32[16,1536]{1,0:T(8,128)S(1)} %pad_maximum_fusion.4), channel_id=1, source_target_pairs={{0,13},{1,4},{2,15},{3,6},{4,1},{5,8},{6,3},{7,10},{8,5},{9,12},{1... | collective-permute-start | bytes 294920 | tf_op jit(solution)/shard_map/ppermute | solution.py:502
  20.4 6.8 %collective-permute-start.3 = (f32[16,2304]{1,0:T(8,128)S(1)}, f32[16,2304]{1,0:T(8,128)S(1)}, u32[]{:S(2)}, u32[]{:S(2)}) collective-permute-start(f32[16,2304]{1,0:T(8,128)S(1)} %pad_maximum_fusion.2), channel_id=1, source_target_pairs={{1,5},{2,14},{3,7},{4,0},{5,9},{6,2},{7,11},{8,4},{9,13},{10,6},{1... | collective-permute-start | bytes 442376 | tf_op jit(solution)/shard_map/ppermute | solution.py:502
  31.5 1.7 %collective-permute-start.4 = (f32[16,4736]{1,0:T(8,128)S(1)}, f32[16,4736]{1,0:T(8,128)S(1)}, u32[]{:S(2)}, u32[]{:S(2)}) collective-permute-start(f32[16,4736]{1,0:T(8,128)S(1)} %get-tuple-element.39.refs_0_), channel_id=1, source_target_pairs={{0,1},{1,0},{2,3},{3,2},{4,5},{5,4},{6,7},{7,6},{8,9},{9,8},{10,11... | collective-permute-start | bytes 909320 | tf_op jit(solution)/shard_map/ppermute | solution.py:502
  33.2 3.5 %collective-permute-start.5 = (f32[16,5376]{1,0:T(8,128)S(1)}, f32[16,5376]{1,0:T(8,128)S(1)}, u32[]{:S(2)}, u32[]{:S(2)}) collective-permute-start(f32[16,5376]{1,0:T(8,128)S(1)} %pad_maximum_fusion.1), channel_id=1, source_target_pairs={{1,2},{2,1},{3,4},{4,3},{5,6},{6,5},{7,8},{8,7},{9,10},{10,9},{11,... | collective-permute-start | bytes 1032200 | tf_op jit(solution)/shard_map/ppermute | solution.py:502
  36.7 14.4 %collective-permute-start.7 = (f32[16,2048]{1,0:T(8,128)S(1)}, f32[16,2048]{1,0:T(8,128)S(1)}, u32[]{:S(2)}, u32[]{:S(2)}) collective-permute-start(f32[16,2048]{1,0:T(8,128)S(1)} %pad_maximum_fusion.3), channel_id=1, source_target_pairs={{1,5},{2,14},{3,7},{4,0},{5,9},{6,2},{7,11},{8,4},{9,13},{10,6},{1... | collective-permute-start | bytes 393224 | tf_op jit(solution)/shard_map/ppermute | solution.py:502
  43.5 7.7 %collective-permute-start.6 = (f32[16,1280]{1,0:T(8,128)S(1)}, f32[16,1280]{1,0:T(8,128)S(1)}, u32[]{:S(2)}, u32[]{:S(2)}) collective-permute-start(f32[16,1280]{1,0:T(8,128)S(1)} %pad_maximum_fusion.5), channel_id=1, source_target_pairs={{0,13},{1,4},{2,15},{3,6},{4,1},{5,8},{6,3},{7,10},{8,5},{9,12},{1... | collective-permute-start | bytes 245768 | tf_op jit(solution)/shard_map/ppermute | solution.py:502
  51.9 6.0 %collective-permute-start.8 = (f32[16,128]{1,0:T(8,128)S(1)}, f32[16,128]{1,0:T(8,128)S(1)}, u32[]{:S(2)}, u32[]{:S(2)}) collective-permute-start(f32[16,128]{1,0:T(8,128)S(1)} %get-tuple-element.44), channel_id=1, source_target_pairs={{0,11},{1,9},{2,8},{3,12},{4,15},{5,10},{6,14},{7,13},{8,1},{9,2},... | collective-permute-start | bytes 24584 | tf_op jit(solution)/shard_map/ppermute | solution.py:502

commit v2 on v1

--- a/solution.py
+++ b/solution.py
@@ -78,10 +78,10 @@
     for which in range(2):
         here = block != 0 if which else block == 0
         live = jnp.where(here & (near >= 0), 1.0, 0.0)
-        counts = sum(live[k:k + 1] for k in range(near.shape[0]))
+        counts = sum(live[k:k + 1] for k in range(1, near.shape[0]))
         first = jnp.sum(jnp.where(across < down, counts, 0.0), axis=1, keepdims=True)
         found = jnp.zeros((clusters, LANES), F32)
-        for k in range(near.shape[0]):
+        for k in range(1, near.shape[0]):
             alive = upright(live[k:k + 1])
             hit = jnp.where(row == first, alive, 0.0)
             found = found + hit * (target * 64 + upright(place[k:k + 1]))
@@ -161,18 +161,18 @@
         columns_ref[at, k] = jnp.broadcast_to(upright[:, k:k + 1], (cl, LANES))
 
 
-def near_block(columns, source, cl, out_ref, at):
+def near_block(columns, source, cl, out_ref):
     for h in range(cl // LANES):
         lanes = slice(h * LANES, (h + 1) * LANES)
         gap = [columns[k] - source(k, h) for k in range(3)]
         square = gap[0] * gap[0] + gap[1] * gap[1] + gap[2] * gap[2]
         high, low = split(lax.rsqrt(square + SMOOTHING))
-        out_ref[at, 0:cl, lanes] = high
-        out_ref[at, cl:2 * cl, lanes] = low
-
-
-def near_product(pieces, block_ref, at, cl):
-    return dot_nt(pieces, block_ref[at, 0:cl, :]) + dot_nt(pieces, block_ref[at, cl:2 * cl, :])
+        out_ref[0:cl, lanes] = high
+        out_ref[cl:2 * cl, lanes] = low
+
+
+def near_product(pieces, block_ref, cl):
+    return dot_nt(pieces, block_ref[0:cl, :]) + dot_nt(pieces, block_ref[cl:2 * cl, :])
 
 
 def fill_charges(pieces_ref, blocks, clusters, cl):
@@ -190,49 +190,40 @@
 def near_kernel(cl, which, number, pairs_ref, *refs):
     blocks = refs[:number]
     if which:
-        columns_ref, start_ref, even_ref, odd_ref, near_out_ref, pieces_ref, sources_ref, total_ref = refs[number:]
+        columns_ref, start_ref, kept_ref, near_out_ref, pieces_ref, sources_ref, total_ref = refs[number:]
     else:
-        _, even_ref, odd_ref, near_out_ref, columns_ref, tail_ref, pieces_ref, sources_ref, total_ref = refs[number:]
+        _, own_ref, kept_ref, near_out_ref, columns_ref, tail_ref, pieces_ref, sources_ref, total_ref = refs[number:]
         tail_ref[...] = blocks[0][:, blocks[0].shape[1] - tail_ref.shape[1]:]
     panels = near_out_ref.shape[1]
     clusters = panels // cl
-    steps = (pairs_ref[2 + which, 0] + 1) // 2
+    group = kept_ref.shape[1]
+    fill_charges(pieces_ref, blocks, clusters, cl)
+    if which:
+        total_ref[...] = jnp.zeros_like(total_ref)
+    else:
+        for c in range(clusters):
+            columns_of(blocks[0], panels, c, cl, columns_ref, c)
+            source = lambda k, h: blocks[0][c:c + 1, panels + k * cl + h * LANES:panels + k * cl + (h + 1) * LANES]
+            near_block([columns_ref[c, k] for k in range(3)], source, cl, own_ref.at[c])
+            total_ref[c] = near_product(pieces_ref[c], own_ref.at[c], cl)
     sources_ref[number * clusters] = jnp.zeros_like(sources_ref[0])
     for b, ref in enumerate(blocks):
         for c in range(clusters):
             for k in range(3):
                 sources_ref[b * clusters + c, k:k + 1, :] = ref[c:c + 1, panels + k * cl:panels + (k + 1) * cl]
-    fill_charges(pieces_ref, blocks, clusters, cl)
-    for c in range(clusters):
-        if not which:
-            columns_of(blocks[0], panels, c, cl, columns_ref, c)
-        total_ref[c] = jnp.zeros_like(total_ref[c])
-    odd_ref[0] = jnp.zeros_like(odd_ref[0])
-
-    def build(ref, at, i):
-        c, j = pair_at(pairs_ref, which, i)
-        source = lambda k, h: sources_ref[j, k:k + 1, h * LANES:(h + 1) * LANES]
-        near_block([columns_ref[c, k] for k in range(3)], source, cl, ref, at)
-
-    def product(ref, at, i):
-        return near_product(pieces_ref[pair_at(pairs_ref, which, i)[1]], ref, at, cl)
-
-    def add(i, part):
-        total_ref[pair_at(pairs_ref, which, i)[0]] += part
 
     def step(m, _):
-        before = jnp.maximum(2 * m - 1, 0)
-        part = product(odd_ref, m, before)
-        build(even_ref, m, 2 * m)
-        add(before, part)
-        part = product(even_ref, m, 2 * m)
-        build(odd_ref, m + 1, 2 * m + 1)
-        add(2 * m, part)
+        pairs = [pair_at(pairs_ref, which, group * m + w) for w in range(group)]
+        parts = []
+        for w, (c, j) in enumerate(pairs):
+            source = lambda k, h: sources_ref[j, k:k + 1, h * LANES:(h + 1) * LANES]
+            near_block([columns_ref[c, k] for k in range(3)], source, cl, kept_ref.at[m, w])
+            parts.append(near_product(pieces_ref[j], kept_ref.at[m, w], cl))
+        for (c, j), part in zip(pairs, parts):
+            total_ref[c] += part
         return 0
 
-    lax.fori_loop(0, steps, step, 0)
-    last = jnp.maximum(2 * steps - 1, 0)
-    add(last, product(odd_ref, steps, last))
+    lax.fori_loop(0, (pairs_ref[2 + which, 0] + group - 1) // group, step, 0)
     for c in range(clusters):
         lanes = slice(c * cl, (c + 1) * cl)
         near = folded(total_ref[c])
@@ -242,27 +233,27 @@
 def near_again_kernel(cl, which, number, pairs_ref, *refs):
     blocks = refs[:number]
     if which:
-        start_ref, even_ref, odd_ref, near_out_ref, pieces_ref, total_ref = refs[number:]
+        start_ref, kept_ref, near_out_ref, pieces_ref, total_ref = refs[number:]
     else:
-        _, even_ref, odd_ref, near_out_ref, tail_ref, pieces_ref, total_ref = refs[number:]
+        _, own_ref, kept_ref, near_out_ref, tail_ref, pieces_ref, total_ref = refs[number:]
         tail_ref[...] = blocks[0][:, blocks[0].shape[1] - tail_ref.shape[1]:]
     clusters = near_out_ref.shape[1] // cl
+    group = kept_ref.shape[1]
     fill_charges(pieces_ref, blocks, clusters, cl)
-    for c in range(clusters):
-        total_ref[c] = jnp.zeros_like(total_ref[c])
-    count = pairs_ref[2 + which, 0]
+    if which:
+        total_ref[...] = jnp.zeros_like(total_ref)
+    else:
+        for c in range(clusters):
+            total_ref[c] = near_product(pieces_ref[c], own_ref.at[c], cl)
 
     def step(m, _):
-        parts = []
-        for w in range(4):
-            i = 4 * m + w
-            at = jnp.where(i < count, i // 2, 0) + w % 2
-            parts.append(near_product(pieces_ref[pair_at(pairs_ref, which, i)[1]], (even_ref, odd_ref)[w % 2], at, cl))
-        for w in range(4):
-            total_ref[pair_at(pairs_ref, which, 4 * m + w)[0]] += parts[w]
+        pairs = [pair_at(pairs_ref, which, group * m + w) for w in range(group)]
+        parts = [near_product(pieces_ref[j], kept_ref.at[m, w], cl) for w, (c, j) in enumerate(pairs)]
+        for (c, j), part in zip(pairs, parts):
+            total_ref[c] += part
         return 0
 
-    lax.fori_loop(0, (count + 3) // 4, step, 0)
+    lax.fori_loop(0, (pairs_ref[2 + which, 0] + group - 1) // group, step, 0)
     for c in range(clusters):
         lanes = slice(c * cl, (c + 1) * cl)
         near = folded(total_ref[c])
@@ -536,8 +527,9 @@
     partner, other, two = exchange(payload, panels + 3 * cl, width)
     total = pltpu.VMEM((clusters, 2 * rhs, cl), F32)
 
-    def kept(most):
-        return [(((most + 1) // 2 + 1, 2 * cl, cl), BF16)] * 2
+    group = 4
+    own = ((clusters, 2 * cl, cl), BF16)
+    kept = ((clusters * (slots - 1) // group, group, 2 * cl, cl), BF16)
 
     def pieces(number):
         return pltpu.VMEM((number * clusters + 1, 2 * rhs, cl), BF16)
@@ -545,20 +537,20 @@
     def sources(number):
         return pltpu.VMEM((number * clusters + 1, 8, cl), F32)
 
-    even, odd, near, columns, tail = call(
+    own_blocks, blocks, near, columns, tail = call(
         functools.partial(near_kernel, cl, 0, 1),
-        [*kept(clusters * slots), whole, ((clusters, 3, cl, LANES), F32), ((rhs, width), F32)],
+        [own, kept, whole, ((clusters, 3, cl, LANES), F32), ((rhs, width), F32)],
         [pieces(1), sources(1), total],
         "svv>ppvpv",
         pairs, payload, partner,
         us=6.0,
     )
     three = last_exchange(tail, [], other)
-    even_other, odd_other, near = call(
+    blocks_other, near = call(
         functools.partial(near_kernel, cl, 1, 2),
-        [*kept(clusters * (slots - 1)), whole],
+        [kept, whole],
         [pieces(2), sources(2), total],
-        "svvpv>ppv",
+        "svvpv>pv",
         pairs, partner, other, columns, near,
         us=4.0,
     )
@@ -580,7 +572,7 @@
         [whole, ((rhs, span + LANES), F32)],
         [pieces(1), total],
         "svvpp>vv",
-        pairs, payload, partner, even, odd,
+        pairs, payload, partner, own_blocks, blocks,
         us=2.5,
     )
     three = last_exchange(tail, [partner[:, panels + span:]], other)
@@ -588,8 +580,8 @@
         functools.partial(near_again_kernel, cl, 1, 2),
         [whole],
         [pieces(2), total],
-        "svvvpp>v",
-        pairs, partner, other, near, even_other, odd_other,
+        "svvvp>v",
+        pairs, partner, other, near, blocks_other,
         us=2.0,
     )
     sums_shape = ((rhs, LANES), F32)

time: 59.6 us -> 57.9 us (0.971)
  Pallas kernels: 24 us -> 20.6 us
  starting transfers between devices: 24.2 us -> 27.3 us
  waiting for transfers between devices: 10 us -> 8.15 us
    pallas_call x9, Pallas kernels: 24 us -> 20.6 us  [call(): pl.pallas_call(kernel, out_shape=[pltpu.VMEM(*out) if m == 'p' else jax.S...]
    ppermute x9, starting transfers between devices: 24.2 us -> 27.3 us  [move(): return lax.ppermute(value, 'clus', pairs)]
    ppermute x9, waiting for transfers between devices: 10 us -> 8.15 us  [move(): return lax.ppermute(value, 'clus', pairs)]
  transfers between devices with their start and end apart: 9 -> 9, of which waited for: 4 -> 4; matrix products, arithmetic and copies ran while one was open for 0% -> 0% of each run, Pallas kernels for 27% -> 22%
where the time goes in v2:
time: 57.9 us; the launch traced here: 57 us
  starting transfers between devices  27.3 us (47%)
  Pallas kernels  20.6 us (36%)
  waiting for transfers between devices  8.15 us (14%)
  between operations  0.79 us (1%)
    ppermute x9, starting transfers between devices, move(): return lax.ppermute(value, 'clus', pairs)  27.3 us
    pallas_call x9, Pallas kernels, call(): pl.pallas_call(kernel, out_shape=[pltpu.VMEM(*out) if m == 'p' else jax.S...  20.6 us
    ppermute x9, waiting for transfers between devices, move(): return lax.ppermute(value, 'clus', pairs)  8.15 us
  transfers between devices with their start and end apart: 9, of which 4 were waited for; matrix products, arithmetic and copies ran while one was open for 0% of the time, Pallas kernels for 22%

profile of v2, /device:TPU:0, one launch (start us, length us, event | category | flops | bytes accessed | tf_op | source)
XLA Modules:
  0.0 57.0 jit_solution(10125821859461926796)
XLA Ops:
  0.6 1.8 %shard_map.95 = (f32[16,5632]{1,0:T(8,128)S(1)}, f32[16,256]{1,0:T(8,128)S(1)}, f32[16,384]{1,0:T(8,128)S(1)}, s32[16,32]{1,0:T(8,128)S(1)}, s32[8,128]{1,0:T(8,...) custom-call(s32[1]{0:T(128)} %bitcast.position_ref, ...), custom_call_target="tpu_custom_call" | custom-call | flops 750000000 | bytes 5400000 | tf_op jit(solution)/shard_map/pallas_call | solution.py:457
  2.4 0.5 collective-permute-start
  3.0 1.3 %collective-permute-done.refs_1_.refs_0_ = f32[16,5632]{1,0:T(8,128)S(1)} collective-permute-done((f32[16,5632]{1,0:T(8,128)S(1)}, f32[16,5632]{1,0:T(8,128)S(1)}, u32[]{:S(2)}, u32[]{:S(2)}) %collective-permute-start) | collective-permute-done | bytes 360480 | tf_op jit(solution)/shard_map/ppermute | solution.py:493
  4.3 0.7 %collective-permute-start.2 = (f32[16,6400]{1,0:T(8,128)S(1)}, f32[16,6400]{1,0:T(8,128)S(1)}, u32[]{:S(2)}, u32[]{:S(2)}) collective-permute-start(f32[16,6400]{1,0:T(8,128)S(1)} %pad_maximum_fusion), channel_id=1, source_target_pairs={{1,2},{2,1},{3,4},{4,3},{5,6},{6,5},{7,8},{8,7},{9,10},{10,9},{11,... | collective-permute-start | bytes 1228808 | tf_op jit(solution)/shard_map/ppermute | solution.py:493
  5.0 7.5 %collective-permute-start.1 = (f32[16,1536]{1,0:T(8,128)S(1)}, f32[16,1536]{1,0:T(8,128)S(1)}, u32[]{:S(2)}, u32[]{:S(2)}) collective-permute-start(f32[16,1536]{1,0:T(8,128)S(1)} %pad_maximum_fusion.4), channel_id=1, source_target_pairs={{0,13},{1,4},{2,15},{3,6},{4,1},{5,8},{6,3},{7,10},{8,5},{9,12},{1... | collective-permute-start | bytes 294920 | tf_op jit(solution)/shard_map/ppermute | solution.py:493
  12.5 5.3 %shard_map.96 = (bf16[16,512,256]{2,1,0:T(8,128)(2,1)S(1)}, bf16[12,4,512,256]{3,2,1,0:T(8,128)(2,1)S(1)}, f32[16,4096]{1,0:T(8,128)S(1)}, f32[16,3,256,128]{3,2,1,0:T(8,128)S(1)}, f32[16,768]{1,0:T(8,128)S(1)}) custom-call(s32[8,128]{1,0:T(8,128)S(1)} %get-tuple-element.26.pairs_ref, f32[16,5632]{1,0:T(8,128)S(1)} %get-tuple-element.28.refs_0_, ...), custom_call_target="tpu_custom_call" | custom-call | flops 3000000000 | bytes 21600000 | tf_op jit(solution)/shard_map/pallas_call | solution.py:457
  17.8 0.0 collective-permute-done.2.refs_1_.other_ref
  17.9 0.5 collective-permute-start.3
  18.4 1.6 %shard_map.97 = (bf16[12,4,512,256]{3,2,1,0:T(8,128)(2,1)S(1)}, f32[16,4096]{1,0:T(8,128)S(1)}) custom-call(s32[8,128]{1,0:T(8,128)S(1)} %get-tuple-element.26.pairs_ref, f32[16,5632]{1,0:T(8,128)S(1)} %collective-permute-done.refs_1_.refs_0_, f32[16,6400]{1,0:T(8,128)S(1)} %collective-permute-done.2.refs_1_.other_ref, ...), custom_call_target="tpu_custom_call" | custom-call | flops 2000000000 | bytes 14400000 | tf_op jit(solution)/shard_map/pallas_call | solution.py:457
  19.9 0.0 collective-permute-done.1.second_ref
  20.0 3.1 %collective-permute-done.3.third_ref = f32[16,2304]{1,0:T(8,128)S(1)} collective-permute-done((f32[16,2304]{1,0:T(8,128)S(1)}, f32[16,2304]{1,0:T(8,128)S(1)}, u32[]{:S(2)}, u32[]{:S(2)}) %collective-permute-start.3) | collective-permute-done | bytes 147488 | tf_op jit(solution)/shard_map/ppermute | solution.py:493
  23.1 4.3 %shard_map.98 = (f32[16,4096]{1,0:T(8,128)S(1)}, f32[16,4736]{1,0:T(8,128)S(1)}, bf16[16,64,1024]{2,1,0:T(8,128)(2,1)S(1)}) custom-call(s32[16,32]{1,0:T(8,128)S(1)} %get-tuple-element.27.at_ref, f32[16,1536]{1,0:T(8,128)S(1)} %collective-permute-done.1.second_ref, f32[16,6400]{1,0:T(8,128)S(1)} %collective-permute-done.2.refs_1_.other_ref, ...), custom_call_target="tpu_custom_call" | custom-call | flops 2249999872 | bytes 16200000 | tf_op jit(solution)/shard_map/pallas_call | solution.py:457
  27.4 2.8 %collective-permute-start.4 = (f32[16,4736]{1,0:T(8,128)S(1)}, f32[16,4736]{1,0:T(8,128)S(1)}, u32[]{:S(2)}, u32[]{:S(2)}) collective-permute-start(f32[16,4736]{1,0:T(8,128)S(1)} %get-tuple-element.38.refs_0_), channel_id=1, source_target_pairs={{0,1},{1,0},{2,3},{3,2},{4,5},{5,4},{6,7},{7,6},{8,9},{9,8},{10,11... | collective-permute-start | bytes 909320 | tf_op jit(solution)/shard_map/ppermute | solution.py:493
  30.1 1.2 %collective-permute-done.4.refs_1_.refs_0_ = f32[16,4736]{1,0:T(8,128)S(1)} collective-permute-done((f32[16,4736]{1,0:T(8,128)S(1)}, f32[16,4736]{1,0:T(8,128)S(1)}, u32[]{:S(2)}, u32[]{:S(2)}) %collective-permute-start.4) | collective-permute-done | bytes 303136 | tf_op jit(solution)/shard_map/ppermute | solution.py:493
  31.4 0.7 %collective-permute-start.5 = (f32[16,5376]{1,0:T(8,128)S(1)}, f32[16,5376]{1,0:T(8,128)S(1)}, u32[]{:S(2)}, u32[]{:S(2)}) collective-permute-start(f32[16,5376]{1,0:T(8,128)S(1)} %pad_maximum_fusion.1), channel_id=1, source_target_pairs={{1,2},{2,1},{3,4},{4,3},{5,6},{6,5},{7,8},{8,7},{9,10},{10,9},{11,... | collective-permute-start | bytes 1032200 | tf_op jit(solution)/shard_map/ppermute | solution.py:493
  32.1 2.4 %shard_map.99 = (f32[16,4096]{1,0:T(8,128)S(1)}, f32[16,640]{1,0:T(8,128)S(1)}) custom-call(s32[8,128]{1,0:T(8,128)S(1)} %get-tuple-element.26.pairs_ref, f32[16,4736]{1,0:T(8,128)S(1)} %get-tuple-element.38.refs_0_, f32[16,4736]{1,0:T(8,128)S(1)} %collective-permute-done.4.refs_1_.refs_0_, bf16[16,512,256]{2,1,0:T(8,128)(2,1)S(1)} %get-tuple-element.39.refs_2_, ...), custom_call_target="tpu_custom_call" | custom-call | flops 1250000000 | bytes 9000000 | tf_op jit(solution)/shard_map/pallas_call | solution.py:457
  34.5 0.0 collective-permute-done.5.refs_2_.refs_1_.other_ref
  34.5 6.9 %collective-permute-start.7 = (f32[16,2048]{1,0:T(8,128)S(1)}, f32[16,2048]{1,0:T(8,128)S(1)}, u32[]{:S(2)}, u32[]{:S(2)}) collective-permute-start(f32[16,2048]{1,0:T(8,128)S(1)} %pad_maximum_fusion.3), channel_id=1, source_target_pairs={{1,5},{2,14},{3,7},{4,0},{5,9},{6,2},{7,11},{8,4},{9,13},{10,6},{1... | collective-permute-start | bytes 393224 | tf_op jit(solution)/shard_map/ppermute | solution.py:493
  41.5 4.9 %collective-permute-start.6 = (f32[16,1280]{1,0:T(8,128)S(1)}, f32[16,1280]{1,0:T(8,128)S(1)}, u32[]{:S(2)}, u32[]{:S(2)}) collective-permute-start(f32[16,1280]{1,0:T(8,128)S(1)} %pad_maximum_fusion.5), channel_id=1, source_target_pairs={{0,13},{1,4},{2,15},{3,6},{4,1},{5,8},{6,3},{7,10},{8,5},{9,12},{1... | collective-permute-start | bytes 245768 | tf_op jit(solution)/shard_map/ppermute | solution.py:493
  46.4 1.2 %shard_map.101.near_ref = f32[16,4096]{1,0:T(8,128)S(1)} custom-call(s32[8,128]{1,0:T(8,128)S(1)} %get-tuple-element.26.pairs_ref, f32[16,4736]{1,0:T(8,128)S(1)} %collective-permute-done.4.refs_1_.refs_0_, f32[16,5376]{1,0:T(8,128)S(1)} %collective-permute-done.5.refs_2_.refs_1_.other_ref, f32[16,4096]{1,0:T(8,128)S(1)} %get-tuple-element.45.refs_2_, ...), custom_call_target="tpu_custom_call" | custom-call | flops 1000000000 | bytes 7200000 | tf_op jit(solution)/shard_map/pallas_call | solution.py:457
  47.5 2.5 %collective-permute-done.6.refs_3_.second_ref = f32[16,1280]{1,0:T(8,128)S(1)} collective-permute-done((f32[16,1280]{1,0:T(8,128)S(1)}, f32[16,1280]{1,0:T(8,128)S(1)}, u32[]{:S(2)}, u32[]{:S(2)}) %collective-permute-start.6) | collective-permute-done | bytes 81952 | tf_op jit(solution)/shard_map/ppermute | solution.py:493
  50.0 0.0 collective-permute-done.7.refs_4_.third_ref
  50.0 0.7 %shard_map.100 = (f32[16,128]{1,0:T(8,128)S(1)}, f32[16,128]{1,0:T(8,128)S(1)}) custom-call(f32[8,128]{1,0:T(8,128)S(1)} %get-tuple-element.25.weights_ref, f32[16,640]{1,0:T(8,128)S(1)} %get-tuple-element.41.refs_0_, f32[16,4736]{1,0:T(8,128)S(1)} %collective-permute-done.4.refs_1_.refs_0_, f32[16,5376]{1,0:T(8,128)S(1)} %collective-permute-done.5.refs_2_.refs_1_.other_ref, ...), custom_call_target="tpu_custom_call" | custom-call | flops 150000000 | bytes 1080000 | tf_op jit(solution)/shard_map/pallas_call | solution.py:457
  50.8 2.9 %collective-permute-start.8 = (f32[16,128]{1,0:T(8,128)S(1)}, f32[16,128]{1,0:T(8,128)S(1)}, u32[]{:S(2)}, u32[]{:S(2)}) collective-permute-start(f32[16,128]{1,0:T(8,128)S(1)} %get-tuple-element.43), channel_id=1, source_target_pairs={{0,11},{1,9},{2,8},{3,12},{4,15},{5,10},{6,14},{7,13},{8,1},{9,2},... | collective-permute-start | bytes 24584 | tf_op jit(solution)/shard_map/ppermute | solution.py:493
  53.6 2.2 %shard_map.102.again_ref = f32[16,4096]{1,0:T(8,128)S(1)} custom-call(s32[16,32]{1,0:T(8,128)S(1)} %get-tuple-element.27.at_ref, f32[16,1280]{1,0:T(8,128)S(1)} %collective-permute-done.6.refs_3_.second_ref, f32[16,5376]{1,0:T(8,128)S(1)} %collective-permute-done.5.refs_2_.refs_1_.other_ref, f32[16,2048]{1,0:T(8,128)S(1)} %collective-permute-done.7.refs_4_.third_ref, ...), custom_call_target="tpu_custom_call" | custom-call | flops 1000000000 | bytes 7200000 | tf_op jit(solution)/shard_map/pallas_call | solution.py:457
  55.8 0.0 collective-permute-done.8.two_ref
  55.8 1.2 %shard_map.103 = (f32[16,4096]{1,0:T(8,128)}, f32[16,4096]{1,0:T(8,128)}) custom-call(f32[16,128]{1,0:T(8,128)S(1)} %get-tuple-element.42.one_ref, f32[16,128]{1,0:T(8,128)S(1)} %collective-permute-done.8.two_ref, f32[16,4096]{1,0:T(8,128)S(1)} %get-tuple-element.44.image_ref, f32[16,4096]{1,0:T(8,128)S(1)} %shard_map.102.again_ref, ...), custom_call_target="tpu_custom_call" | custom-call | flops 500000000 | bytes 3600000 | tf_op jit(solution)/shard_map/pallas_call | solution.py:457
  (13 shorter events, 0.1 us)
Async XLA Ops:
  2.4 1.8 %collective-permute-start = (f32[16,5632]{1,0:T(8,128)S(1)}, f32[16,5632]{1,0:T(8,128)S(1)}, u32[]{:S(2)}, u32[]{:S(2)}) collective-permute-start(f32[16,5632]{1,0:T(8,128)S(1)} %get-tuple-element.28.refs_0_), channel_id=1, source_target_pairs={{0,1},{1,0},{2,3},{3,2},{4,5},{5,4},{6,7},{7,6},{8,9},{9,8},{10,11... | collective-permute-start | bytes 1081352 | tf_op jit(solution)/shard_map/ppermute | solution.py:493
  4.3 13.5 %collective-permute-start.2 = (f32[16,6400]{1,0:T(8,128)S(1)}, f32[16,6400]{1,0:T(8,128)S(1)}, u32[]{:S(2)}, u32[]{:S(2)}) collective-permute-start(f32[16,6400]{1,0:T(8,128)S(1)} %pad_maximum_fusion), channel_id=1, source_target_pairs={{1,2},{2,1},{3,4},{4,3},{5,6},{6,5},{7,8},{8,7},{9,10},{10,9},{11,... | collective-permute-start | bytes 1228808 | tf_op jit(solution)/shard_map/ppermute | solution.py:493
  5.0 14.9 %collective-permute-start.1 = (f32[16,1536]{1,0:T(8,128)S(1)}, f32[16,1536]{1,0:T(8,128)S(1)}, u32[]{:S(2)}, u32[]{:S(2)}) collective-permute-start(f32[16,1536]{1,0:T(8,128)S(1)} %pad_maximum_fusion.4), channel_id=1, source_target_pairs={{0,13},{1,4},{2,15},{3,6},{4,1},{5,8},{6,3},{7,10},{8,5},{9,12},{1... | collective-permute-start | bytes 294920 | tf_op jit(solution)/shard_map/ppermute | solution.py:493
  17.9 5.2 %collective-permute-start.3 = (f32[16,2304]{1,0:T(8,128)S(1)}, f32[16,2304]{1,0:T(8,128)S(1)}, u32[]{:S(2)}, u32[]{:S(2)}) collective-permute-start(f32[16,2304]{1,0:T(8,128)S(1)} %pad_maximum_fusion.2), channel_id=1, source_target_pairs={{1,5},{2,14},{3,7},{4,0},{5,9},{6,2},{7,11},{8,4},{9,13},{10,6},{1... | collective-permute-start | bytes 442376 | tf_op jit(solution)/shard_map/ppermute | solution.py:493
  27.4 4.0 %collective-permute-start.4 = (f32[16,4736]{1,0:T(8,128)S(1)}, f32[16,4736]{1,0:T(8,128)S(1)}, u32[]{:S(2)}, u32[]{:S(2)}) collective-permute-start(f32[16,4736]{1,0:T(8,128)S(1)} %get-tuple-element.38.refs_0_), channel_id=1, source_target_pairs={{0,1},{1,0},{2,3},{3,2},{4,5},{5,4},{6,7},{7,6},{8,9},{9,8},{10,11... | collective-permute-start | bytes 909320 | tf_op jit(solution)/shard_map/ppermute | solution.py:493
  31.4 3.1 %collective-permute-start.5 = (f32[16,5376]{1,0:T(8,128)S(1)}, f32[16,5376]{1,0:T(8,128)S(1)}, u32[]{:S(2)}, u32[]{:S(2)}) collective-permute-start(f32[16,5376]{1,0:T(8,128)S(1)} %pad_maximum_fusion.1), channel_id=1, source_target_pairs={{1,2},{2,1},{3,4},{4,3},{5,6},{6,5},{7,8},{8,7},{9,10},{10,9},{11,... | collective-permute-start | bytes 1032200 | tf_op jit(solution)/shard_map/ppermute | solution.py:493
  34.5 15.5 %collective-permute-start.7 = (f32[16,2048]{1,0:T(8,128)S(1)}, f32[16,2048]{1,0:T(8,128)S(1)}, u32[]{:S(2)}, u32[]{:S(2)}) collective-permute-start(f32[16,2048]{1,0:T(8,128)S(1)} %pad_maximum_fusion.3), channel_id=1, source_target_pairs={{1,5},{2,14},{3,7},{4,0},{5,9},{6,2},{7,11},{8,4},{9,13},{10,6},{1... | collective-permute-start | bytes 393224 | tf_op jit(solution)/shard_map/ppermute | solution.py:493
  41.5 8.6 %collective-permute-start.6 = (f32[16,1280]{1,0:T(8,128)S(1)}, f32[16,1280]{1,0:T(8,128)S(1)}, u32[]{:S(2)}, u32[]{:S(2)}) collective-permute-start(f32[16,1280]{1,0:T(8,128)S(1)} %pad_maximum_fusion.5), channel_id=1, source_target_pairs={{0,13},{1,4},{2,15},{3,6},{4,1},{5,8},{6,3},{7,10},{8,5},{9,12},{1... | collective-permute-start | bytes 245768 | tf_op jit(solution)/shard_map/ppermute | solution.py:493
  50.8 5.1 %collective-permute-start.8 = (f32[16,128]{1,0:T(8,128)S(1)}, f32[16,128]{1,0:T(8,128)S(1)}, u32[]{:S(2)}, u32[]{:S(2)}) collective-permute-start(f32[16,128]{1,0:T(8,128)S(1)} %get-tuple-element.43), channel_id=1, source_target_pairs={{0,11},{1,9},{2,8},{3,12},{4,15},{5,10},{6,14},{7,13},{8,1},{9,2},... | collective-permute-start | bytes 24584 | tf_op jit(solution)/shard_map/ppermute | solution.py:493

commit v3 on v2

--- a/solution.py
+++ b/solution.py
@@ -92,12 +92,12 @@
     return out.astype(jnp.int32)
 
 
-def prepare_kernel(cl, vcl, rank, position_ref, vertices_hbm, corners_hbm, krylov_hbm, basis_hbm, far_hbm, near_hbm, offsets_hbm, weights_hbm,
-                   payload_ref, area_ref, center_ref, at_ref, pairs_ref, basis_ref, krylov_ref, offsets_ref, weights_ref,
+def prepare_kernel(cl, vcl, rank, position_ref, vertices_hbm, corners_hbm, krylov_hbm, basis_hbm, far_hbm, near_hbm, offsets_hbm,
+                   payload_ref, heavy_ref, area_ref, center_ref, at_ref, pairs_ref, basis_ref, krylov_ref, offsets_ref,
                    vertices_ref, corners_ref, raw_ref, far_ref, near_ref, mesh_ref, local_ref, sems):
     moves = copies((
         (vertices_hbm, vertices_ref), (corners_hbm, corners_ref), (krylov_hbm, krylov_ref), (basis_hbm, raw_ref),
-        (far_hbm, far_ref), (near_hbm, near_ref), (offsets_hbm, offsets_ref), (weights_hbm.at[position_ref[0]], weights_ref),
+        (far_hbm, far_ref), (near_hbm, near_ref), (offsets_hbm, offsets_ref),
     ), sems)
     rhs, panels = krylov_ref.shape
     clusters = panels // cl
@@ -116,7 +116,9 @@
         corner = [[jnp.take_along_axis(tables[k], local[m], axis=1, mode="promise_in_bounds") for k in range(3)] for m in range(3)]
         for k in range(3):
             middle = (corner[0][k] + corner[1][k] + corner[2][k]) / 3.0
-            payload_ref[:, panels + k * cl + h * LANES:panels + k * cl + (h + 1) * LANES] = middle
+            lanes = slice(panels + k * cl + h * LANES, panels + k * cl + (h + 1) * LANES)
+            payload_ref[:, lanes] = middle
+            heavy_ref[:, lanes] = middle
             sums[k] = middle if h == 0 else sums[k] + middle
         one = [corner[1][k] - corner[0][k] for k in range(3)]
         two = [corner[2][k] - corner[0][k] for k in range(3)]
@@ -140,6 +142,7 @@
         basis_ref[:, lanes] = stacked(raw_ref[:, lanes])
         charges = area_ref[c:c + 1, :] * krylov_ref[:, lanes]
         payload_ref[:, lanes] = charges
+        heavy_ref[:, lanes] = charges
         payload_ref[:, table + c * rank:table + (c + 1) * rank] = moments_of(charges, basis_ref[:, lanes])
     moves[4].wait()
     far = far_ref[...]
@@ -151,7 +154,6 @@
     moves[5].wait()
     pairs_ref[...] = pair_list(near_ref[...], position_ref[0], clusters)
     moves[6].wait()
-    moves[7].wait()
 
 
 def columns_of(payload_ref, panels, c, cl, columns_ref, at):
@@ -278,12 +280,9 @@
                 middle_ref[s * count + at] = pltpu.roll(tile, s * rank, 1) if s else tile
 
 
-def six_tables(width, second_ref, other_ref, third_ref):
-    gap = third_ref.shape[1] - 3 * width
-    return (
-        (second_ref, width), (second_ref, 0), (other_ref, other_ref.shape[1] - width),
-        (third_ref, 2 * width + gap), (third_ref, width + gap), (third_ref, 0),
-    )
+def six_tables(near_ref, far_ref, swapped_ref):
+    width = near_ref.shape[1] // 2
+    return (far_ref, 0), (far_ref, width), (near_ref, 0), (swapped_ref, width), (swapped_ref, 0), (swapped_ref, 3 * width)
 
 
 def pick(source_ref, at_ref, c, g, per, lane):
@@ -304,13 +303,13 @@
     return folded(dot_nn(fields_ref[c], basis))
 
 
-def image_kernel(cl, rank, at_ref, second_ref, other_ref, third_ref, center_ref, area_ref, near_ref, basis_ref, krylov_ref, offsets_ref,
-                 image_ref, payload_ref, coupling_ref, pieces_ref, middle_ref, gathered_ref, fields_ref):
+def image_kernel(cl, rank, at_ref, near_pair_ref, far_pair_ref, swapped_ref, center_ref, area_ref, near_ref, basis_ref, krylov_ref, offsets_ref,
+                 image_ref, payload_ref, heavy_ref, coupling_ref, pieces_ref, middle_ref, gathered_ref, fields_ref):
     rhs, panels = near_ref.shape
     clusters = panels // cl
     per = LANES // rank
     span = clusters * rank
-    load_window(six_tables(span + span // 2, second_ref, other_ref, third_ref), clusters, rank, pieces_ref, middle_ref)
+    load_window(six_tables(near_pair_ref, far_pair_ref, swapped_ref), clusters, rank, pieces_ref, middle_ref)
     lane = lax.broadcasted_iota(jnp.int32, (1, LANES), 1) // rank
     for c in range(clusters):
         mine = [offsets_ref[3, k:k + 1, :] - center_ref[c:c + 1, k * LANES:(k + 1) * LANES] for k in range(3)]
@@ -332,6 +331,7 @@
         charges = area * image
         image_ref[:, lanes] = image
         payload_ref[:, lanes] = charges
+        heavy_ref[:, lanes] = charges
         payload_ref[:, panels + c * rank:panels + (c + 1) * rank] = moments_of(charges, basis)
         krylov = krylov_ref[:, lanes]
         squared = squared + krylov * krylov
@@ -343,11 +343,11 @@
     payload_ref[:, panels + span:] = in_lanes(squared, correlation, jnp.sum(residual * residual, axis=1, keepdims=True), local)
 
 
-def far_again_kernel(cl, rank, at_ref, second_ref, other_ref, third_ref, near_ref, area_ref, coupling_ref, basis_ref,
+def far_again_kernel(cl, rank, at_ref, near_pair_ref, far_pair_ref, swapped_ref, near_ref, area_ref, coupling_ref, basis_ref,
                      image_ref, pieces_ref, gathered_ref, fields_ref):
     clusters = near_ref.shape[1] // cl
     per = LANES // rank
-    load_window(six_tables(clusters * rank + LANES, second_ref, other_ref, third_ref), clusters, rank, pieces_ref, None)
+    load_window(six_tables(near_pair_ref, far_pair_ref, swapped_ref), clusters, rank, pieces_ref, None)
     lane = lax.broadcasted_iota(jnp.int32, (1, LANES), 1) // rank
     for c in range(clusters):
         for g in range(at_ref.shape[1] // per):
@@ -389,65 +389,26 @@
     return out
 
 
-def merged(groups, weights=None):
-    weights = weights or [1.0] * len(groups)
-    squared = sum(weight * group[:, 0:1] for group, weight in zip(groups, weights))
-    correlation = sum(weight * group[:, 1:2] for group, weight in zip(groups, weights))
+def merged(groups):
+    squared = sum(group[:, 0:1] for group in groups)
+    correlation = sum(group[:, 1:2] for group in groups)
     local = ratio(correlation, squared)
     energy = 0.0
-    for group, weight in zip(groups, weights):
+    for group in groups:
         gap = local - group[:, 3:4]
-        energy = energy + weight * (group[:, 2:3] + gap * gap * group[:, 0:1])
+        energy = energy + (group[:, 2:3] + gap * gap * group[:, 0:1])
     return squared, correlation, energy, local
 
 
-def known_sums(tail_ref, partner_ref, other_ref, second_ref, third_ref):
-    width = tail_ref.shape[1]
-    ends = [(tail_ref, width), (partner_ref, partner_ref.shape[1]), (other_ref, other_ref.shape[1] - width), (other_ref, other_ref.shape[1])]
-    ends += [(second_ref, width), (second_ref, 2 * width)]
-    ends += [(third_ref, width), (third_ref, width + LANES), (third_ref, 2 * width + LANES), (third_ref, 3 * width + LANES)]
-    return [ref[:, end - LANES:end] for ref, end in ends]
-
-
-def known_sums_kernel(weights_ref, *refs):
-    groups = known_sums(*refs[:5])
-    for side, out_ref in enumerate(refs[5:]):
-        weights = [weights_ref[0:1, 16 * side + i:16 * side + i + 1] for i in range(len(groups))]
-        out_ref[...] = in_lanes(*merged(groups, weights))
-
-
-def completing(devices, *moves):
-    partner, other, second, third = ({target: source for source, target in move} for move in moves)
-    slots = []
-    for i in range(devices):
-        two, three = second[i], third[i]
-        slots.append([i, partner[i], other[i], partner[other[i]], two, partner[two], three, partner[three], other[three], partner[other[three]]])
-    known = [set(slot) for slot in slots]
-    everyone = set(range(devices))
-    target_of = {}
-
-    def matched(target, seen):
-        for source in range(devices):
-            if source not in seen and known[target] | known[source] == everyone:
-                seen.add(source)
-                if source not in target_of or matched(target_of[source], seen):
-                    target_of[source] = target
-                    return True
-        return False
-
-    if not all(matched(i, set()) for i in range(devices)):
-        return None
-    weights = np.zeros((devices, 8, LANES), np.float32)
-    for i in range(devices):
-        for at, device in enumerate(slots[i]):
-            if device not in slots[i][:at]:
-                weights[i, :, at] = 1.0
-                weights[i, :, 16 + at] = device not in known[target_of[i]]
-    return sorted(target_of.items()), weights
+def window_sums_kernel(payload_ref, partner_ref, near_pair_ref, far_pair_ref, swapped_ref, out_ref):
+    width = near_pair_ref.shape[1] // 2
+    ends = [(payload_ref, payload_ref.shape[1]), (partner_ref, partner_ref.shape[1])]
+    ends += [(ref, end) for ref in (near_pair_ref, far_pair_ref, swapped_ref) for end in (width, 2 * width)]
+    out_ref[...] = in_lanes(*merged([ref[:, end - LANES:end] for ref, end in ends]))
 
 
 def merge_kernel(one_ref, two_ref, out_ref):
-    out_ref[...] = in_lanes(*merged([ref[:, ref.shape[1] - LANES:] for ref in (one_ref, two_ref)]))
+    out_ref[...] = in_lanes(*merged([one_ref[...], two_ref[...]]))
 
 
 def call(kernel, outs, scratch, memory, *args, limit=6, us=1.0):
@@ -482,33 +443,28 @@
     width = span + span // 2
     pairing = [(i, i + 1 - 2 * (i % 2)) for i in range(devices)]
     bridging = [(i, i - 1 + 2 * (i % 2)) for i in range(1, devices - 1)] + [(0, 0), (devices - 1, devices - 1)]
-    second = [(i, (i + 3 * (2 * (i % 2) - 1)) % devices) for i in range(devices)]
-    third = [(i, i + 4 * (2 * (i % 2) - 1)) for i in range(1, devices - 1)] + [(0, 3), (devices - 1, devices - 4)]
-    third = [(i, j % devices) for i, j in third]
-
-    completion = completing(devices, pairing, bridging, second, third)
-    weights = completion[1] if completion else np.zeros((devices, 8, LANES), np.float32)
 
     def move(value, pairs):
         return lax.ppermute(value, "clus", pairs)
 
-    def exchange(value, first, width):
-        mine = value[:, first:first + width]
-        partner = move(value, pairing)
-        pair = jnp.concatenate([mine, partner[:, first:first + width]], axis=1)
-        other = move(jnp.concatenate([value[:, :first], pair], axis=1), bridging)
-        return partner, other, move(pair, second)
-
-    def last_exchange(tail, between, other):
-        pair = other[:, other.shape[1] - 2 * tail.shape[1]:]
-        return move(jnp.concatenate([tail, *between, pair], axis=1), third)
+    def outward(value, steps):
+        return move(value, [(i, (i + steps * (1 - 2 * (i % 2))) % devices) for i in range(devices)])
+
+    def exchange(payload, heavy):
+        other = move(heavy, bridging)
+        partner = move(payload, pairing)
+        pair = jnp.concatenate([value[:, heavy.shape[1]:] for value in (payload, partner)], axis=1)
+        return partner, other, outward(pair, 2), outward(pair, 4)
+
+    def swapped(near_pair, far_pair, tail):
+        return move(jnp.concatenate([near_pair, far_pair, tail], axis=1), pairing)
 
     whole = ((rhs, panels), F32)
-    payload, area, centers, at, pairs, basis, krylov, offsets, weights = call(
+    payload, heavy, area, centers, at, pairs, basis, krylov, offsets = call(
         functools.partial(prepare_kernel, cl, vcl, rank),
         [
-            ((rhs, panels + 3 * cl + width), F32), ((clusters, cl), F32), ((clusters, 3 * LANES), F32),
-            (far_pairs.shape, jnp.int32), ((8, LANES), jnp.int32), ((2 * rank, panels), BF16), whole, (offsets.shape, F32), ((8, LANES), F32),
+            ((rhs, panels + 3 * cl + width), F32), ((rhs, panels + 3 * cl), F32), ((clusters, cl), F32), ((clusters, 3 * LANES), F32),
+            (far_pairs.shape, jnp.int32), ((8, LANES), jnp.int32), ((2 * rank, panels), BF16), whole, (offsets.shape, F32),
         ],
         [
             pltpu.VMEM(vertices.shape, F32),
@@ -518,13 +474,13 @@
             pltpu.VMEM((slots, clusters), jnp.int32),
             pltpu.VMEM((3 * clusters, vcl), F32),
             pltpu.VMEM((3 * panels // LANES, LANES), jnp.int32),
-            pltpu.SemaphoreType.DMA((8,)),
+            pltpu.SemaphoreType.DMA((7,)),
         ],
-        "shhhhhhhh>vvvvvpppp",
-        position, vertices, panel_vertices, krylov, basis, far_pairs, near_pairs.T, offsets, jnp.asarray(weights),
+        "shhhhhhh>vvvvvvppp",
+        position, vertices, panel_vertices, krylov, basis, far_pairs, near_pairs.T, offsets,
         us=1.5,
     )
-    partner, other, two = exchange(payload, panels + 3 * cl, width)
+    partner, other, near_pair, far_pair = exchange(payload, heavy)
     total = pltpu.VMEM((clusters, 2 * rhs, cl), F32)
 
     group = 4
@@ -539,13 +495,13 @@
 
     own_blocks, blocks, near, columns, tail = call(
         functools.partial(near_kernel, cl, 0, 1),
-        [own, kept, whole, ((clusters, 3, cl, LANES), F32), ((rhs, width), F32)],
+        [own, kept, whole, ((clusters, 3, cl, LANES), F32), ((rhs, LANES), F32)],
         [pieces(1), sources(1), total],
         "svv>ppvpv",
         pairs, payload, partner,
-        us=6.0,
-    )
-    three = last_exchange(tail, [], other)
+        us=8.0,
+    )
+    swap = swapped(near_pair, far_pair, tail)
     blocks_other, near = call(
         functools.partial(near_kernel, cl, 1, 2),
         [kept, whole],
@@ -558,24 +514,24 @@
     window = pltpu.VMEM((tiles, 2 * rhs, LANES), BF16)
     gathered = pltpu.VMEM((clusters, 2 * rhs, partners * rank), BF16)
     fields = pltpu.VMEM((clusters, 2 * rhs, 2 * rank), BF16)
-    image, payload, coupling = call(
+    image, payload, heavy, coupling = call(
         functools.partial(image_kernel, cl, rank),
-        [whole, ((rhs, panels + span + LANES), F32), ((clusters, 2 * rank, partners * rank), BF16)],
+        [whole, ((rhs, panels + span + LANES), F32), whole, ((clusters, 2 * rank, partners * rank), BF16)],
         [window, pltpu.VMEM((tiles, 8, LANES), F32), gathered, fields],
-        "svvvvvvppp>vvp",
-        at, two, other, three, centers, area, near, basis, krylov, offsets,
+        "svvvvvvppp>vvvp",
+        at, near_pair, far_pair, swap, centers, area, near, basis, krylov, offsets,
         us=4.5,
     )
-    partner, other, two = exchange(payload, panels, span + LANES)
+    partner, other, near_pair, far_pair = exchange(payload, heavy)
     near, tail = call(
         functools.partial(near_again_kernel, cl, 0, 1),
-        [whole, ((rhs, span + LANES), F32)],
+        [whole, ((rhs, LANES), F32)],
         [pieces(1), total],
         "svvpp>vv",
         pairs, payload, partner, own_blocks, blocks,
-        us=2.5,
-    )
-    three = last_exchange(tail, [partner[:, panels + span:]], other)
+        us=8.0,
+    )
+    swap = swapped(near_pair, far_pair, tail)
     (near,) = call(
         functools.partial(near_again_kernel, cl, 1, 2),
         [whole],
@@ -585,21 +541,19 @@
         us=2.0,
     )
     sums_shape = ((rhs, LANES), F32)
-    if completion:
-        one, many = call(known_sums_kernel, [sums_shape] * 2, [], "pvvvvv>vv", weights, tail, partner, other, two, three, us=0.3)
-        many = move(many, completion[0])
-    else:
-        one, many, size = tail, partner, 2
-        while size < devices:
-            (one,) = call(merge_kernel, [sums_shape], [], "vv>v", one, many, us=0.3)
-            many = move(one, [(i, (i + size) % devices) for i in range(devices)])
-            size = 2 * size
+    (one,) = call(window_sums_kernel, [sums_shape], [], "vvvvv>v", payload, partner, near_pair, far_pair, swap, us=0.3)
+    size = 8
+    many = outward(one, size)
+    while 2 * size < devices:
+        (one,) = call(merge_kernel, [sums_shape], [], "vv>v", one, many, us=0.3)
+        size = 2 * size
+        many = outward(one, size)
     (again,) = call(
         functools.partial(far_again_kernel, cl, rank),
         [whole],
         [window, gathered, fields],
         "svvvvvpp>v",
-        at, two, other, three, near, area, coupling, basis,
+        at, near_pair, far_pair, swap, near, area, coupling, basis,
         us=2.0,
     )
     here = pltpu.VMEM((rhs, panels), F32)

time: 57.9 us -> 48.3 us (0.83); the launches traced: 57 us -> 48.7 us
  starting transfers between devices: 27.3 us -> 10 us
  Pallas kernels: 20.6 us -> 26.4 us
  waiting for transfers between devices: 8.15 us -> 11.4 us
    ppermute x9 -> x11, starting transfers between devices: 27.3 us -> 10 us  [move(): return lax.ppermute(value, 'clus', pairs)]
    pallas_call x9, Pallas kernels: 20.6 us -> 26.4 us  [call(): pl.pallas_call(kernel, out_shape=[pltpu.VMEM(*out) if m == 'p' else jax.S...]
    ppermute x9 -> x11, waiting for transfers between devices: 8.15 us -> 11.4 us  [move(): return lax.ppermute(value, 'clus', pairs)]
  transfers between devices with their start and end apart: 9 -> 11, of which waited for: 4 -> 6; matrix products, arithmetic and copies ran while one was open for 0% -> 0% of each run, Pallas kernels for 22% -> 39%
where the time goes in v3:
time: 48.3 us; the launch traced here: 48.7 us
  Pallas kernels  26.4 us (55%)
  waiting for transfers between devices  11.4 us (24%)
  starting transfers between devices  10 us (21%)
  between operations  0.8 us (2%)
    pallas_call x9, Pallas kernels, call(): pl.pallas_call(kernel, out_shape=[pltpu.VMEM(*out) if m == 'p' else jax.S...  26.4 us
    ppermute x11, waiting for transfers between devices, move(): return lax.ppermute(value, 'clus', pairs)  11.4 us
    ppermute x11, starting transfers between devices, move(): return lax.ppermute(value, 'clus', pairs)  10 us
  transfers between devices with their start and end apart: 11, of which 6 were waited for; matrix products, arithmetic and copies ran while one was open for 0% of the time, Pallas kernels for 39%

profile of v3, /device:TPU:0, one launch (start us, length us, event | category | flops | bytes accessed | tf_op | source)
XLA Modules:
  0.0 48.7 jit_solution(11697708846983263895)
XLA Ops:
  0.6 1.8 %shard_map.86 = (f32[16,5632]{1,0:T(8,128)S(1)}, f32[16,4864]{1,0:T(8,128)S(1)}, f32[16,256]{1,0:T(8,128)S(1)}, f32[16,384]{1,0:T(8,128)S(1)}, s32[16,32]{1,0:T(...) custom-call(s32[1]{0:T(128)} %bitcast.position_ref, ...), custom_call_target="tpu_custom_call" | custom-call | flops 750000000 | bytes 5400000 | tf_op jit(solution)/shard_map/pallas_call | solution.py:418
  2.4 0.5 %collective-permute-start = (f32[16,5632]{1,0:T(8,128)S(1)}, f32[16,5632]{1,0:T(8,128)S(1)}, u32[]{:S(2)}, u32[]{:S(2)}) collective-permute-start(f32[16,5632]{1,0:T(8,128)S(1)} %get-tuple-element.25.refs_0_), channel_id=1, source_target_pairs={{0,1},{1,0},{2,3},{3,2},{4,5},{5,4},{6,7},{7,6},{8,9},{9,8},{10,11... | collective-permute-start | bytes 1081352 | tf_op jit(solution)/shard_map/ppermute | solution.py:448
  3.0 0.7 %collective-permute-start.4 = (f32[16,4864]{1,0:T(8,128)S(1)}, f32[16,4864]{1,0:T(8,128)S(1)}, u32[]{:S(2)}, u32[]{:S(2)}) collective-permute-start(f32[16,4864]{1,0:T(8,128)S(1)} %get-tuple-element.30), channel_id=1, source_target_pairs={{1,2},{2,1},{3,4},{4,3},{5,6},{6,5},{7,8},{8,7},{9,10},{10,9},{11,... | collective-permute-start | bytes 933896 | tf_op jit(solution)/shard_map/ppermute | solution.py:448
  3.6 0.6 %collective-permute-done.refs_1_.refs_0_ = f32[16,5632]{1,0:T(8,128)S(1)} collective-permute-done((f32[16,5632]{1,0:T(8,128)S(1)}, f32[16,5632]{1,0:T(8,128)S(1)}, u32[]{:S(2)}, u32[]{:S(2)}) %collective-permute-start) | collective-permute-done | bytes 360480 | tf_op jit(solution)/shard_map/ppermute | solution.py:448
  4.3 3.2 %collective-permute-start.1 = (f32[16,1536]{1,0:T(8,128)S(1)}, f32[16,1536]{1,0:T(8,128)S(1)}, u32[]{:S(2)}, u32[]{:S(2)}) collective-permute-start(f32[16,1536]{1,0:T(8,128)S(1)} %pad_maximum_fusion.2), channel_id=1, source_target_pairs={{0,2},{1,15},{2,4},{3,1},{4,6},{5,3},{6,8},{7,5},{8,10},{9,7},{10,... | collective-permute-start | bytes 294920 | tf_op jit(solution)/shard_map/ppermute | solution.py:448
  7.5 2.2 %collective-permute-start.2 = (f32[16,1536]{1,0:T(8,128)S(1)}, f32[16,1536]{1,0:T(8,128)S(1)}, u32[]{:S(2)}, u32[]{:S(2)}) collective-permute-start(f32[16,1536]{1,0:T(8,128)S(1)} %pad_maximum_fusion.2), channel_id=1, source_target_pairs={{0,4},{1,13},{2,6},{3,15},{4,8},{5,1},{6,10},{7,3},{8,12},{9,5},{1... | collective-permute-start | bytes 294920 | tf_op jit(solution)/shard_map/ppermute | solution.py:448
  9.7 6.9 %shard_map.87 = (bf16[16,512,256]{2,1,0:T(8,128)(2,1)S(1)}, bf16[12,4,512,256]{3,2,1,0:T(8,128)(2,1)S(1)}, f32[16,4096]{1,0:T(8,128)S(1)}, f32[16,3,256,128]{3,2,1,0:T(8,128)S(1)}, f32[16,128]{1,0:T(8,128)S(1)}) custom-call(s32[8,128]{1,0:T(8,128)S(1)} %get-tuple-element.26.pairs_ref, f32[16,5632]{1,0:T(8,128)S(1)} %get-tuple-element.25.refs_0_, ...), custom_call_target="tpu_custom_call" | custom-call | flops 4000000000 | bytes 28800000 | tf_op jit(solution)/shard_map/pallas_call | solution.py:418
  16.6 0.0 collective-permute-done.1.near_pair_ref
  16.6 2.4 %collective-permute-done.2.far_pair_ref = f32[16,1536]{1,0:T(8,128)S(1)} collective-permute-done((f32[16,1536]{1,0:T(8,128)S(1)}, f32[16,1536]{1,0:T(8,128)S(1)}, u32[]{:S(2)}, u32[]{:S(2)}) %collective-permute-start.2) | collective-permute-done | bytes 98336 | tf_op jit(solution)/shard_map/ppermute | solution.py:448
  19.0 0.1 collective-permute-start.3
  19.1 0.0 collective-permute-done.4.refs_1_
  19.1 4.0 %shard_map.88 = (bf16[12,4,512,256]{3,2,1,0:T(8,128)(2,1)S(1)}, f32[16,4096]{1,0:T(8,128)S(1)}) custom-call(s32[8,128]{1,0:T(8,128)S(1)} %get-tuple-element.26.pairs_ref, f32[16,5632]{1,0:T(8,128)S(1)} %collective-permute-done.refs_1_.refs_0_, f32[16,4864]{1,0:T(8,128)S(1)} %collective-permute-done.4.refs_1_, ...), custom_call_target="tpu_custom_call" | custom-call | flops 2000000000 | bytes 14400000 | tf_op jit(solution)/shard_map/pallas_call | solution.py:418
  23.2 0.0 collective-permute-done.3.swapped_ref
  23.2 4.3 %shard_map.89 = (f32[16,4096]{1,0:T(8,128)S(1)}, f32[16,4736]{1,0:T(8,128)S(1)}, f32[16,4096]{1,0:T(8,128)S(1)}, bf16[16,64,1024]{2,1,0:T(8,128)(2,1)S(1)}) custom-call(s32[16,32]{1,0:T(8,128)S(1)} %get-tuple-element.24.at_ref, f32[16,1536]{1,0:T(8,128)S(1)} %collective-permute-done.1.near_pair_ref, f32[16,1536]{1,0:T(8,128)S(1)} %collective-permute-done.2.far_pair_ref, ...), custom_call_target="tpu_custom_call" | custom-call | flops 2249999872 | bytes 16200000 | tf_op jit(solution)/shard_map/pallas_call | solution.py:418
  27.5 0.1 collective-permute-start.5
  27.6 0.7 %collective-permute-start.10 = (f32[16,4096]{1,0:T(8,128)S(1)}, f32[16,4096]{1,0:T(8,128)S(1)}, u32[]{:S(2)}, u32[]{:S(2)}) collective-permute-start(f32[16,4096]{1,0:T(8,128)S(1)} %get-tuple-element.42), channel_id=1, source_target_pairs={{1,2},{2,1},{3,4},{4,3},{5,6},{6,5},{7,8},{8,7},{9,10},{10,9},{11,... | collective-permute-start | bytes 786440 | tf_op jit(solution)/shard_map/ppermute | solution.py:448
  28.3 0.9 %collective-permute-done.5.refs_1_.partner_ref.refs_0_ = f32[16,4736]{1,0:T(8,128)S(1)} collective-permute-done((f32[16,4736]{1,0:T(8,128)S(1)}, f32[16,4736]{1,0:T(8,128)S(1)}, u32[]{:S(2)}, u32[]{:S(2)}) %collective-permute-start.5) | collective-permute-done | bytes 303136 | tf_op jit(solution)/shard_map/ppermute | solution.py:448
  29.2 2.5 %collective-permute-start.6 = (f32[16,1280]{1,0:T(8,128)S(1)}, f32[16,1280]{1,0:T(8,128)S(1)}, u32[]{:S(2)}, u32[]{:S(2)}) collective-permute-start(f32[16,1280]{1,0:T(8,128)S(1)} %pad_maximum_fusion.3), channel_id=1, source_target_pairs={{0,2},{1,15},{2,4},{3,1},{4,6},{5,3},{6,8},{7,5},{8,10},{9,7},{10,... | collective-permute-start | bytes 245768 | tf_op jit(solution)/shard_map/ppermute | solution.py:448
  31.7 0.0 collective-permute-start.7
  31.7 3.2 %shard_map.90 = (f32[16,4096]{1,0:T(8,128)S(1)}, f32[16,128]{1,0:T(8,128)S(1)}) custom-call(s32[8,128]{1,0:T(8,128)S(1)} %get-tuple-element.26.pairs_ref, f32[16,4736]{1,0:T(8,128)S(1)} %get-tuple-element.37.refs_0_.payload_ref, f32[16,4736]{1,0:T(8,128)S(1)} %collective-permute-done.5.refs_1_.partner_ref.refs_0_, ...), custom_call_target="tpu_custom_call" | custom-call | flops 4000000000 | bytes 28800000 | tf_op jit(solution)/shard_map/pallas_call | solution.py:418
  34.9 1.9 %collective-permute-done.6.near_pair_ref = f32[16,1280]{1,0:T(8,128)S(1)} collective-permute-done((f32[16,1280]{1,0:T(8,128)S(1)}, f32[16,1280]{1,0:T(8,128)S(1)}, u32[]{:S(2)}, u32[]{:S(2)}) %collective-permute-start.6) | collective-permute-done | bytes 81952 | tf_op jit(solution)/shard_map/ppermute | solution.py:448
  36.9 3.2 %collective-permute-done.7.far_pair_ref = f32[16,1280]{1,0:T(8,128)S(1)} collective-permute-done((f32[16,1280]{1,0:T(8,128)S(1)}, f32[16,1280]{1,0:T(8,128)S(1)}, u32[]{:S(2)}, u32[]{:S(2)}) %collective-permute-start.7) | collective-permute-done | bytes 81952 | tf_op jit(solution)/shard_map/ppermute | solution.py:448
  40.1 0.1 collective-permute-start.8
  40.2 0.0 collective-permute-done.10.refs_1_
  40.2 2.4 %shard_map.92.near_ref = f32[16,4096]{1,0:T(8,128)S(1)} custom-call(s32[8,128]{1,0:T(8,128)S(1)} %get-tuple-element.26.pairs_ref, f32[16,4736]{1,0:T(8,128)S(1)} %collective-permute-done.5.refs_1_.partner_ref.refs_0_, f32[16,4096]{1,0:T(8,128)S(1)} %collective-permute-done.10.refs_1_, f32[16,4096]{1,0:T(8,128)S(1)} %get-tuple-element.43.refs_2_, ...), custom_call_target="tpu_custom_call" | custom-call | flops 1000000000 | bytes 7200000 | tf_op jit(solution)/shard_map/pallas_call | solution.py:418
  42.6 0.0 collective-permute-done.8.swapped_ref
  42.6 0.3 shard_map.91.one_ref
  42.9 0.0 collective-permute-start.9
  42.9 2.2 %shard_map.93.again_ref = f32[16,4096]{1,0:T(8,128)S(1)} custom-call(s32[16,32]{1,0:T(8,128)S(1)} %get-tuple-element.24.at_ref, f32[16,1280]{1,0:T(8,128)S(1)} %collective-permute-done.6.near_pair_ref, f32[16,1280]{1,0:T(8,128)S(1)} %collective-permute-done.7.far_pair_ref, f32[16,2688]{1,0:T(8,128)S(1)} %collective-permute-done.8.swapped_ref, ...), custom_call_target="tpu_custom_call" | custom-call | flops 1000000000 | bytes 7200000 | tf_op jit(solution)/shard_map/pallas_call | solution.py:418
  45.1 2.4 %collective-permute-done.9.two_ref = f32[16,128]{1,0:T(8,128)S(1)} collective-permute-done((f32[16,128]{1,0:T(8,128)S(1)}, f32[16,128]{1,0:T(8,128)S(1)}, u32[]{:S(2)}, u32[]{:S(2)}) %collective-permute-start.9) | collective-permute-done | bytes 8224 | tf_op jit(solution)/shard_map/ppermute | solution.py:448
  47.5 1.2 %shard_map.94 = (f32[16,4096]{1,0:T(8,128)}, f32[16,4096]{1,0:T(8,128)}) custom-call(f32[16,128]{1,0:T(8,128)S(1)} %shard_map.91.one_ref, f32[16,128]{1,0:T(8,128)S(1)} %collective-permute-done.9.two_ref, f32[16,4096]{1,0:T(8,128)S(1)} %get-tuple-element.41.image_ref, f32[16,4096]{1,0:T(8,128)S(1)} %shard_map.93.again_ref, ...), custom_call_target="tpu_custom_call" | custom-call | flops 500000000 | bytes 3600000 | tf_op jit(solution)/shard_map/pallas_call | solution.py:418
  (8 shorter events, 0.1 us)
Async XLA Ops:
  2.4 1.8 %collective-permute-start = (f32[16,5632]{1,0:T(8,128)S(1)}, f32[16,5632]{1,0:T(8,128)S(1)}, u32[]{:S(2)}, u32[]{:S(2)}) collective-permute-start(f32[16,5632]{1,0:T(8,128)S(1)} %get-tuple-element.25.refs_0_), channel_id=1, source_target_pairs={{0,1},{1,0},{2,3},{3,2},{4,5},{5,4},{6,7},{7,6},{8,9},{9,8},{10,11... | collective-permute-start | bytes 1081352 | tf_op jit(solution)/shard_map/ppermute | solution.py:448
  3.0 16.2 %collective-permute-start.4 = (f32[16,4864]{1,0:T(8,128)S(1)}, f32[16,4864]{1,0:T(8,128)S(1)}, u32[]{:S(2)}, u32[]{:S(2)}) collective-permute-start(f32[16,4864]{1,0:T(8,128)S(1)} %get-tuple-element.30), channel_id=1, source_target_pairs={{1,2},{2,1},{3,4},{4,3},{5,6},{6,5},{7,8},{8,7},{9,10},{10,9},{11,... | collective-permute-start | bytes 933896 | tf_op jit(solution)/shard_map/ppermute | solution.py:448
  4.3 12.3 %collective-permute-start.1 = (f32[16,1536]{1,0:T(8,128)S(1)}, f32[16,1536]{1,0:T(8,128)S(1)}, u32[]{:S(2)}, u32[]{:S(2)}) collective-permute-start(f32[16,1536]{1,0:T(8,128)S(1)} %pad_maximum_fusion.2), channel_id=1, source_target_pairs={{0,2},{1,15},{2,4},{3,1},{4,6},{5,3},{6,8},{7,5},{8,10},{9,7},{10,... | collective-permute-start | bytes 294920 | tf_op jit(solution)/shard_map/ppermute | solution.py:448
  7.5 11.5 %collective-permute-start.2 = (f32[16,1536]{1,0:T(8,128)S(1)}, f32[16,1536]{1,0:T(8,128)S(1)}, u32[]{:S(2)}, u32[]{:S(2)}) collective-permute-start(f32[16,1536]{1,0:T(8,128)S(1)} %pad_maximum_fusion.2), channel_id=1, source_target_pairs={{0,4},{1,13},{2,6},{3,15},{4,8},{5,1},{6,10},{7,3},{8,12},{9,5},{1... | collective-permute-start | bytes 294920 | tf_op jit(solution)/shard_map/ppermute | solution.py:448
  19.0 4.1 %collective-permute-start.3 = (f32[16,3200]{1,0:T(8,128)S(1)}, f32[16,3200]{1,0:T(8,128)S(1)}, u32[]{:S(2)}, u32[]{:S(2)}) collective-permute-start(f32[16,3200]{1,0:T(8,128)S(1)} %pad_maximum_fusion), channel_id=1, source_target_pairs={{0,1},{1,0},{2,3},{3,2},{4,5},{5,4},{6,7},{7,6},{8,9},{9,8},{10,11... | collective-permute-start | bytes 614408 | tf_op jit(solution)/shard_map/ppermute | solution.py:448
  27.5 1.7 %collective-permute-start.5 = (f32[16,4736]{1,0:T(8,128)S(1)}, f32[16,4736]{1,0:T(8,128)S(1)}, u32[]{:S(2)}, u32[]{:S(2)}) collective-permute-start(f32[16,4736]{1,0:T(8,128)S(1)} %get-tuple-element.37.refs_0_.payload_ref), channel_id=1, source_target_pairs={{0,1},{1,0},{2,3},{3,2},{4,5},{5,4},{6,7},{7,6},{8,9},{9,8},{10,11... | collective-permute-start | bytes 909320 | tf_op jit(solution)/shard_map/ppermute | solution.py:448
  27.6 12.6 %collective-permute-start.10 = (f32[16,4096]{1,0:T(8,128)S(1)}, f32[16,4096]{1,0:T(8,128)S(1)}, u32[]{:S(2)}, u32[]{:S(2)}) collective-permute-start(f32[16,4096]{1,0:T(8,128)S(1)} %get-tuple-element.42), channel_id=1, source_target_pairs={{1,2},{2,1},{3,4},{4,3},{5,6},{6,5},{7,8},{8,7},{9,10},{10,9},{11,... | collective-permute-start | bytes 786440 | tf_op jit(solution)/shard_map/ppermute | solution.py:448
  29.2 7.7 %collective-permute-start.6 = (f32[16,1280]{1,0:T(8,128)S(1)}, f32[16,1280]{1,0:T(8,128)S(1)}, u32[]{:S(2)}, u32[]{:S(2)}) collective-permute-start(f32[16,1280]{1,0:T(8,128)S(1)} %pad_maximum_fusion.3), channel_id=1, source_target_pairs={{0,2},{1,15},{2,4},{3,1},{4,6},{5,3},{6,8},{7,5},{8,10},{9,7},{10,... | collective-permute-start | bytes 245768 | tf_op jit(solution)/shard_map/ppermute | solution.py:448
  31.7 8.4 %collective-permute-start.7 = (f32[16,1280]{1,0:T(8,128)S(1)}, f32[16,1280]{1,0:T(8,128)S(1)}, u32[]{:S(2)}, u32[]{:S(2)}) collective-permute-start(f32[16,1280]{1,0:T(8,128)S(1)} %pad_maximum_fusion.3), channel_id=1, source_target_pairs={{0,4},{1,13},{2,6},{3,15},{4,8},{5,1},{6,10},{7,3},{8,12},{9,5},{1... | collective-permute-start | bytes 245768 | tf_op jit(solution)/shard_map/ppermute | solution.py:448
  40.1 2.5 %collective-permute-start.8 = (f32[16,2688]{1,0:T(8,128)S(1)}, f32[16,2688]{1,0:T(8,128)S(1)}, u32[]{:S(2)}, u32[]{:S(2)}) collective-permute-start(f32[16,2688]{1,0:T(8,128)S(1)} %pad_maximum_fusion.1), channel_id=1, source_target_pairs={{0,1},{1,0},{2,3},{3,2},{4,5},{5,4},{6,7},{7,6},{8,9},{9,8},{10,11... | collective-permute-start | bytes 516104 | tf_op jit(solution)/shard_map/ppermute | solution.py:448
  42.9 4.6 %collective-permute-start.9 = (f32[16,128]{1,0:T(8,128)S(1)}, f32[16,128]{1,0:T(8,128)S(1)}, u32[]{:S(2)}, u32[]{:S(2)}) collective-permute-start(f32[16,128]{1,0:T(8,128)S(1)} %shard_map.91.one_ref), channel_id=1, source_target_pairs={{0,8},{1,9},{2,10},{3,11},{4,12},{5,13},{6,14},{7,15},{8,0},{9,1},... | collective-permute-start | bytes 24584 | tf_op jit(solution)/shard_map/ppermute | solution.py:448
